TPU v7x, 32 devices: a whole 2x2x4 slice. The times are simulated.
32 devices in a mesh: patch: 8 (over z, y), visit: 4 (over x, core).
Axes of the slice: x: 2, y: 2, z: 4, core: 2. Of those that a mesh axis runs over, the one named last changes fastest.
Arguments:
- science: float32 [4096, 2, 128], P(('patch', 'visit')), may hold values from -40 to 40
- inverse_sigma: float32 [4096, 2, 128], P(('patch', 'visit')), may hold values from 0.24 to 3.6
- template: float32 [8, 256, 1024], P('patch', 'visit'), may hold values from -6 to 6
- destination: int32 [4096], P(('patch', 'visit')), may hold values from 0 to 7, as said below
- offsets: int32 [4096, 2], P(('patch', 'visit')), may hold values from 0 to 876, as said below
- visit_local: int32 [4096], P(('patch', 'visit')), may hold values from 0 to 15, as said below
Outputs:
- difference: float32 [4096, 2, 128], P(('patch', 'visit'))
- coefficients: float32 [64, 28], P('visit')
Inputs may be any that keep to these rules, and one draw needn't show every extreme that they name: `destination`: in each aligned block of 128 rows no patch is named more than 32 times, and in every draw some patch is named exactly 32 times in every block. `offsets`: column 0 is at most 234, column 1 at most 876. `visit_local`: each aligned block of 128 rows holds every value exactly 128 // 16 times.
All inputs are finite; a program needn't handle non-finite values.
Results may differ from a plain program's by a relative error of at most 0.0098.
Values may be sent and summed in bfloat16 or wider, within the bound.
A program may use at most 64 MiB of HBM per device.

v0:
```python
import math

import jax
import jax.numpy as jnp
import numpy as np
from jax import lax
from jax.sharding import PartitionSpec as P

KR = 10
NF = 11
NB = 28
VIS_DEV = 16


gauss_widths = (1.0, 2.0, 4.0)
poly_degrees = (4, 2, 2)


def as_sent(array):
    return jax.tree.map(lambda a: a.astype(jnp.bfloat16) if a.dtype == jnp.float32 else a, array)


def filter_table(radius):
    tap_points = np.arange(-radius, radius + 1) * 1.0
    raw_columns = []
    for width_value, degree in zip(gauss_widths, poly_degrees):
        bell_curve = np.exp(-tap_points * tap_points / (2.0 * width_value * width_value))
        for power_index in range(degree + 1):
            raw_columns.append(bell_curve * (tap_points / radius) ** power_index)
    orthonormal = []
    for column in raw_columns:
        vector = column.copy()
        for repeat_index in range(2):
            for earlier in orthonormal:
                vector = vector - np.dot(earlier, vector) * earlier
        orthonormal.append(vector / np.sqrt(np.dot(vector, vector)))
    return np.stack(orthonormal, axis=1).astype(np.float32)


def pair_layout():
    column_ids = []
    row_ids = []
    filter_runs = []
    offset = 0
    for degree in poly_degrees:
        for first_index in range(degree + 1):
            filter_runs.append((offset + first_index, offset, offset + degree - first_index + 1))
            for second_index in range(degree + 1 - first_index):
                column_ids.append(offset + first_index)
                row_ids.append(offset + second_index)
        offset += degree + 1
    return (column_ids, row_ids, filter_runs)


def build_tables(row_count, column_count):
    values = filter_table(KR)
    filters = values.shape[1]
    taps_count = 2 * KR + 1
    row_band = np.zeros((filters, row_count, row_count + 2 * KR), np.float32)
    for out_row in range(row_count):
        row_band[:, out_row, out_row : out_row + taps_count] = values.T
    column_band = np.zeros((filters, column_count + 2 * KR, column_count), np.float32)
    for out_column in range(column_count):
        column_band[:, out_column : out_column + taps_count, out_column] = values.T
    row_matrix = jnp.asarray(row_band.reshape(filters * row_count, row_count + 2 * KR)).astype(
        jnp.bfloat16
    )
    column_matrix = jnp.asarray(column_band).astype(jnp.bfloat16)
    tap_values = lax.optimization_barrier(jnp.asarray(values).astype(jnp.bfloat16)).astype(
        jnp.float32
    )
    return (row_matrix, column_matrix, tap_values)


def slice_windows(whole, row_starts, column_starts, height, breadth):

    def one_window(row_at, column_at):
        return lax.dynamic_slice(whole, (row_at, column_at), (height, breadth))

    return jax.vmap(one_window)(row_starts, column_starts)


def filtered_block(windows, row_matrix):
    count_items = windows.shape[0]
    row_count = row_matrix.shape[0] // NF
    product = jnp.einsum("ry,nyx->nrx", row_matrix, windows, preferred_element_type=jnp.float32)
    return product.astype(jnp.bfloat16).reshape(count_items, NF, row_count, windows.shape[2])


def fit_block(
    windows, block_scaled, block_weights, block_visits, block_live, row_matrix, column_matrix
):
    count_items = windows.shape[0]
    filtered = filtered_block(windows, row_matrix)
    column_ids, row_ids, filter_runs = pair_layout()
    pieces_list = []
    for column_id, low_row, high_row in filter_runs:
        pieces_list.append(
            jnp.einsum(
                "nbix,xj->nbij",
                filtered[:, low_row:high_row],
                column_matrix[column_id],
                preferred_element_type=jnp.float32,
            )
        )
    images = jnp.concatenate(pieces_list, axis=1)
    weight_values = block_weights.astype(jnp.float32)
    design = (images * weight_values[:, None]).astype(jnp.bfloat16)
    design = jnp.concatenate([design, block_weights[:, None]], axis=1).reshape(count_items, NB, -1)
    gram_matrix = jnp.einsum("nkp,nlp->nkl", design, design, preferred_element_type=jnp.float32)
    right_vector = jnp.einsum(
        "nkp,np->nk",
        design,
        block_scaled.reshape(count_items, -1),
        preferred_element_type=jnp.float32,
    )
    member = (block_visits[:, None] == jnp.arange(VIS_DEV, dtype=jnp.int32)[None, :]) & (
        block_live[:, None] > 0
    )
    member = jnp.where(member, 1.0, 0.0).astype(jnp.float32)
    gram_visit = jnp.einsum("nv,nkl->vkl", member, gram_matrix, precision=lax.Precision.HIGHEST)
    right_visit = jnp.einsum("nv,nk->vk", member, right_vector, precision=lax.Precision.HIGHEST)
    return (gram_visit, right_visit)


def model_block(windows, block_visits, coefficients, mixing, row_matrix, tap_values):
    filtered = filtered_block(windows, row_matrix)
    column_count = windows.shape[2] - 2 * KR
    combined = jnp.einsum(
        "nab,nbix->naix",
        jnp.take(mixing, block_visits, axis=0),
        filtered.astype(jnp.float32),
        precision=lax.Precision.HIGHEST,
    )
    model = jnp.take(coefficients[:, NB - 1], block_visits)[:, None, None] + jnp.zeros(
        combined.shape[:1] + combined.shape[2:3] + (column_count,), jnp.float32
    )
    for shift_index in range(2 * KR + 1):
        weighted = (
            combined[..., shift_index : shift_index + column_count]
            * tap_values[shift_index][None, :, None, None]
        )
        model = model + jnp.sum(weighted, axis=1)
    return model.astype(jnp.bfloat16)


def in_blocks(function, arrays, block_size):
    total_rows = arrays[0].shape[0]
    shaped = tuple(
        (
            values.reshape((total_rows // block_size, block_size) + values.shape[1:])
            for values in arrays
        )
    )
    return lax.map(lambda pieces: function(*pieces), shaped)


def visit_sums(windows, scaled, weights, visits, live, row_matrix, column_matrix):
    block_size = math.gcd(windows.shape[0], 32)

    def visit_one_block(part_windows, part_scaled, part_weights, part_visits, part_live):
        return fit_block(
            part_windows,
            part_scaled,
            part_weights,
            part_visits,
            part_live,
            row_matrix,
            column_matrix,
        )

    block_gram_list, right_blocks = in_blocks(
        visit_one_block, (windows, scaled, weights, visits, live), block_size
    )
    return (jnp.sum(block_gram_list, axis=0), jnp.sum(right_blocks, axis=0))


def fit_coefficients(gram_total, right_total):
    gram_total, right_total = lax.psum((gram_total, right_total), "patch")
    factor = jnp.linalg.cholesky(gram_total)
    return jax.scipy.linalg.cho_solve((factor, True), right_total[..., None])[..., 0]


def model_all(windows, visits, coefficients, row_matrix, tap_values):
    column_ids, row_ids, filter_runs = pair_layout()
    column_index = jnp.asarray(column_ids, dtype=jnp.int32)
    row_index = jnp.asarray(row_ids, dtype=jnp.int32)
    mixing = (
        jnp.zeros((VIS_DEV, NF, NF), jnp.float32)
        .at[:, column_index, row_index]
        .set(coefficients[:, : NB - 1])
    )
    block_size = math.gcd(windows.shape[0], 32)

    def model_one_block(part_windows, part_visits):
        return model_block(part_windows, part_visits, coefficients, mixing, row_matrix, tap_values)

    model = in_blocks(model_one_block, (windows, visits), block_size)
    return model.reshape((windows.shape[0],) + model.shape[2:])


def per_device(science, inverse_sigma, template, destination, offsets, visit_local):
    patches = lax.axis_size("patch")
    tile_count, row_count, column_count = science.shape
    capacity = max(2, 2 * tile_count // patches)
    slot_count = patches * capacity
    height = row_count + 2 * KR
    breadth = column_count + 2 * KR
    row_matrix, column_matrix, tap_values = build_tables(row_count, column_count)
    gathered = lax.all_gather(template.astype(jnp.bfloat16), "visit", axis=1, tiled=True)
    whole_template = gathered[0]
    order_ids = jnp.arange(tile_count, dtype=jnp.int32)
    same_patch = destination[:, None] == destination[None, :]
    before = order_ids[None, :] < order_ids[:, None]
    tile_rank = jnp.sum(jnp.where(same_patch & before, 1, 0), axis=1).astype(jnp.int32)
    slot_of_tile = destination * capacity + tile_rank
    slot_ids = jnp.arange(slot_count, dtype=jnp.int32)
    holds = slot_of_tile[None, :] == slot_ids[:, None]
    filled = jnp.any(holds, axis=1)
    source_tile = jnp.sum(jnp.where(holds, order_ids[None, :], 0), axis=1)
    weights = inverse_sigma.astype(jnp.bfloat16)
    scaled_science = (science * inverse_sigma).astype(jnp.bfloat16)
    zero_tile = jnp.zeros((), jnp.bfloat16)
    packed_science = jnp.where(
        filled[:, None, None], jnp.take(scaled_science, source_tile, axis=0), zero_tile
    )
    packed_weights = jnp.where(
        filled[:, None, None], jnp.take(weights, source_tile, axis=0), zero_tile
    )
    details = jnp.stack(
        [
            jnp.where(filled, 1, 0).astype(jnp.int32),
            jnp.take(visit_local, source_tile),
            jnp.take(offsets[:, 0], source_tile),
            jnp.take(offsets[:, 1], source_tile),
        ],
        axis=1,
    )
    details = jnp.where(filled[:, None], details, 0)
    arrived_science, arrived_weights, arrived_details = (
        lax.all_to_all(
            packed_science.reshape(patches, capacity, row_count, column_count),
            "patch",
            split_axis=0,
            concat_axis=0,
            tiled=True,
        ),
        lax.all_to_all(
            packed_weights.reshape(patches, capacity, row_count, column_count),
            "patch",
            split_axis=0,
            concat_axis=0,
            tiled=True,
        ),
        lax.all_to_all(
            details.reshape(patches, capacity, 4), "patch", split_axis=0, concat_axis=0, tiled=True
        ),
    )
    arrived_science = arrived_science.reshape(slot_count, row_count, column_count)
    arrived_weights = arrived_weights.reshape(slot_count, row_count, column_count)
    arrived_details = arrived_details.reshape(slot_count, 4)
    windows = slice_windows(
        whole_template, arrived_details[:, 2], arrived_details[:, 3], height, breadth
    )
    gram_total, right_total = visit_sums(
        windows,
        arrived_science,
        arrived_weights,
        arrived_details[:, 1],
        arrived_details[:, 0],
        row_matrix,
        column_matrix,
    )
    coefficients = fit_coefficients(gram_total, right_total)
    model = model_all(windows, arrived_details[:, 1], coefficients, row_matrix, tap_values)
    returned = lax.all_to_all(
        as_sent(model.reshape(patches, capacity, row_count, column_count)),
        "patch",
        split_axis=0,
        concat_axis=0,
        tiled=True,
    )
    own_model = jnp.take(
        returned.reshape(slot_count, row_count, column_count), slot_of_tile, axis=0
    )
    difference = science - lax.optimization_barrier(own_model).astype(jnp.float32)
    return (difference, coefficients)


def solution(mesh):
    return jax.shard_map(
        per_device,
        mesh=mesh,
        in_specs=(
            P(("patch", "visit"), None, None),
            P(("patch", "visit"), None, None),
            P("patch", "visit", None),
            P(("patch", "visit")),
            P(("patch", "visit"), None),
            P(("patch", "visit")),
        ),
        out_specs=(P(("patch", "visit"), None, None), P("visit", None)),
        check_vma=False,
    )
```

profile of v0, /device:TPU:0, one launch (start us, length us, event | category | flops | bytes accessed | tf_op | source)
XLA Modules:
  0.0 974.0 jit_solution(8264949740451343503)
XLA Ops:
  10.1 7.3 all-to-all-start
  17.4 7.2 all_gather.3
  26.6 2.2 broadcast_select_fusion.3
  28.8 6.0 all-to-all-start.1
  36.2 6.1 all-to-all-done.1
  42.3 3.4 all-to-all-start.2
  45.7 661.6 %while.25 = (s32[]{:T(128)}, bf16[256,1024]{1,0:T(8,128)(2,1)S(1)}, s32[256,2]{0,1:T(2,128)S(1)}, bf16[256,22,148]{2,1,0:T(8,128)(2,1)}, s32[]{:T(128)}) while((s32[]{:T(128)}, bf16[256,1024]{1,0:T(8,128)(2,1)S(1)}, s32[256,2]{0,1:T(2,128)S(1)}, bf16[256,22,148]{2,1,0:T(8,128)(2,1)}, s32[]{:T(128)}) %tuple.136), condition=%wide.while_cond, body=%wide.while_body.sunk | while | flops 2 | bytes 20433 | solution.py:78
  69.6 2.0 bitcast_dynamic-update-slice_fusion.2
  72.2 2.0 bitcast_dynamic-update-slice_fusion.2
  85.1 2.0 bitcast_dynamic-update-slice_fusion.2
  95.4 2.0 bitcast_dynamic-update-slice_fusion.2
  100.6 2.0 bitcast_dynamic-update-slice_fusion.2
  108.4 2.0 bitcast_dynamic-update-slice_fusion.2
  121.3 2.0 bitcast_dynamic-update-slice_fusion.2
  123.9 2.0 bitcast_dynamic-update-slice_fusion.2
  134.2 2.0 bitcast_dynamic-update-slice_fusion.2
  142.0 2.0 bitcast_dynamic-update-slice_fusion.2
  154.9 2.0 bitcast_dynamic-update-slice_fusion.2
  165.2 2.0 bitcast_dynamic-update-slice_fusion.2
  193.6 2.0 bitcast_dynamic-update-slice_fusion.2
  258.2 2.0 bitcast_dynamic-update-slice_fusion.2
  289.3 2.0 bitcast_dynamic-update-slice_fusion.2
  307.3 2.0 bitcast_dynamic-update-slice_fusion.2
  361.6 2.0 bitcast_dynamic-update-slice_fusion.2
  397.8 2.0 bitcast_dynamic-update-slice_fusion.2
  423.6 2.0 bitcast_dynamic-update-slice_fusion.2
  444.3 2.0 bitcast_dynamic-update-slice_fusion.2
  457.2 2.0 bitcast_dynamic-update-slice_fusion.2
  485.6 2.0 bitcast_dynamic-update-slice_fusion.2
  493.4 2.0 bitcast_dynamic-update-slice_fusion.2
  498.6 2.0 bitcast_dynamic-update-slice_fusion.2
  506.3 2.0 bitcast_dynamic-update-slice_fusion.2
  537.3 2.0 bitcast_dynamic-update-slice_fusion.2
  547.7 2.0 bitcast_dynamic-update-slice_fusion.2
  568.3 2.0 bitcast_dynamic-update-slice_fusion.2
  591.6 2.0 bitcast_dynamic-update-slice_fusion.2
  617.4 2.0 bitcast_dynamic-update-slice_fusion.2
  632.9 2.0 bitcast_dynamic-update-slice_fusion.2
  638.1 2.0 bitcast_dynamic-update-slice_fusion.2
  692.4 2.0 bitcast_dynamic-update-slice_fusion.2
  707.4 66.2 %while.26 = (s32[]{:T(128)}, f32[8,16,28,28]{3,1,2,0:T(8,128)}, f32[8,16,28]{2,1,0:T(8,128)S(1)}, s32[8,32]{1,0:T(8,128)S(1)}, s32[8,32]{1,0:T(8,128)S(1)}, /*in...) while((s32[]{:T(128)}, f32[8,16,28,28]{3,1,2,0:T(8,128)}, ...), condition=%wide.region_4.7_spmd.clone, body=%wide.region_3.6_spmd.clone.sunk | while | flops 90732320 | bytes 13360773 | solution.py:155
  775.5 41.0 %all-reduce = (f32[16,28]{1,0:T(8,128)S(1)}, f32[16,28,28]{1,2,0:T(8,128)S(1)}) all-reduce(f32[16,28]{1,0:T(8,128)S(1)} %reduce_sum.270, f32[16,28,28]{1,2,0:T(8,128)S(1)} %copy.141), channel_id=1, replica_groups=mesh['patch'=8,'visit'=4] {'patch'}, use_global_device_ids=true, to_apply=%region_10.13 | all-reduce | flops 12992 | bytes 103936 | tf_op jit(solution)/shard_map/psum | solution.py:179
  816.8 41.0 %custom-call.11 = f32[16,28,28]{2,1,0:T(8,128)S(1)} custom-call(f32[16,28,28]{2,1,0:T(8,128)S(1)} %fusion.103), custom_call_target="Cholesky" | custom-call | tf_op jit(solution)/shard_map/jit(cholesky)/cholesky | solution.py:180
  858.1 34.5 %custom-call.12 = f32[16,1,28,28]{2,3,1,0:T(8,128)S(1)} custom-call(f32[16,1,28,28]{3,2,1,0:T(8,128)S(1)} %select_bitcast_fusion.2), custom_call_target="InvertDiagBlocksLowerTriangular" | custom-call | tf_op jit(solution)/shard_map/jit(_cho_solve)/vmap()/triangular_solve | solution.py:181
  893.8 2.2 scatter_fusion
  896.1 65.7 %while.27 = (s32[]{:T(128)}, bf16[8,32,2,128]{3,2,1,0:T(2,128)(2,1)}, s32[8,32]{1,0:T(8,128)S(1)}, f32[16,28]{0,1:T(8,128)S(1)}, f32[16,11,11]{2,1,0:T(8,128)S(1...) while((s32[]{:T(128)}, ...), condition=%wide.region_34.37_spmd.clone, body=%wide.region_12.36_spmd.clone.sunk | while | flops 22240096 | bytes 10662593 | solution.py:155
  961.8 3.4 all-to-all-start.3
  965.2 7.3 all-to-all-done.3
  (1287 shorter events, 743.2 us)
Async XLA Ops:
  0.6 2.0 copy-start
  0.6 28.1 %copy-start.8 = (bf16[21,11]{1,0:T(8,128)(2,1)S(1)}, bf16[21,11]{1,0:T(8,128)(2,1)}, u32[]{:S(2)}) copy-start(bf16[21,11]{1,0:T(8,128)(2,1)} %constant.208) | copy-start | bytes 1390
  0.7 16.7 %copy-start.5 = (f32[1,64,1024]{2,1,0:T(8,128)S(1)}, f32[1,64,1024]{2,1,0:T(8,128)}, u32[]{:S(2)}) copy-start(f32[1,64,1024]{2,1,0:T(8,128)} %param.21) | copy-start | bytes 786436
  0.7 23.9 %copy-start.4 = (f32[128,2,128]{2,1,0:T(2,128)S(1)}, f32[128,2,128]{2,1,0:T(2,128)}, u32[]{:S(2)}) copy-start(f32[128,2,128]{2,1,0:T(2,128)} %param.19) | copy-start | bytes 393220
  0.7 23.9 %copy-start.6 = (f32[128,2,128]{2,1,0:T(2,128)S(1)}, f32[128,2,128]{2,1,0:T(2,128)}, u32[]{:S(2)}) copy-start(f32[128,2,128]{2,1,0:T(2,128)} %param.20) | copy-start | bytes 393220
  2.6 704.8 %copy-start.1 = (bf16[11,148,128]{2,1,0:T(8,128)(2,1)S(1)}, bf16[11,148,128]{2,1,0:T(8,128)(2,1)}, u32[]{:S(2)}) copy-start(bf16[11,148,128]{2,1,0:T(8,128)(2,1)} %constant.198) | copy-start | bytes 1250308
  2.6 704.8 %copy-start.2 = (bf16[22,22,1]{1,0,2:T(8,128)(2,1)S(1)}, bf16[22,22,1]{1,0,2:T(8,128)(2,1)}, u32[]{:S(2)}) copy-start(bf16[22,22,1]{1,0,2:T(8,128)(2,1)} %constant.405) | copy-start | bytes 2908
  10.1 18.7 %all-to-all-start = ((s32[8,1,128]{2,1,0:T(1,128)}), s32[8,1,128]{2,1,0:T(1,128)S(1)}, u32[]{:S(2)}, u32[]{:S(2)}) async-start(s32[8,1,128]{2,1,0:T(1,128)} %reshape.539), calls=%async_computation | async-start | bytes 8192 | tf_op jit(solution)/shard_map/all_to_all | solution.py:255
  28.8 13.5 %all-to-all-start.1 = ((bf16[8,32,2,128]{3,2,1,0:T(2,128)(2,1)}), bf16[8,32,2,128]{3,2,1,0:T(2,128)(2,1)S(1)}, u32[]{:S(2)}, u32[]{:S(2)}) async-start(bf16[8,32,2,128]{3,2,1,0:T(2,128)(2,1)} %bitcast.4), calls=%async_computation.1 | async-start | bytes 262144 | tf_op jit(solution)/shard_map/all_to_all | solution.py:248
  42.3 665.1 %all-to-all-start.2 = ((bf16[8,32,2,128]{3,2,1,0:T(2,128)(2,1)}), bf16[8,32,2,128]{3,2,1,0:T(2,128)(2,1)S(1)}, u32[]{:S(2)}, u32[]{:S(2)}) async-start(bf16[8,32,2,128]{3,2,1,0:T(2,128)(2,1)} %bitcast.5), calls=%async_computation.2 | async-start | bytes 262144 | tf_op jit(solution)/shard_map/all_to_all | solution.py:241
  773.6 120.1 %copy-start.3 = (s32[27]{0:T(128)S(1)}, s32[27]{0:T(128)}, u32[]{:S(2)}) copy-start(s32[27]{0:T(128)} %constant.236) | copy-start | bytes 328
  893.5 2.5 copy-start.7
  961.8 10.7 %all-to-all-start.3 = ((bf16[8,32,2,128]{3,2,1,0:T(2,128)(2,1)}), bf16[8,32,2,128]{3,2,1,0:T(2,128)(2,1)S(1)}, u32[]{:S(2)}, u32[]{:S(2)}) async-start(bf16[8,32,2,128]{3,2,1,0:T(2,128)(2,1)} %get-tuple-element.101), calls=%async_computation.3 | async-start | bytes 262144 | tf_op jit(solution)/shard_map/all_to_all | solution.py:276
where the time goes:
time: 980 us; the launch traced here: 974 us
  local copies, waits for them, and re-layouts  711 us (73%)
  other arithmetic  123 us (13%)
  matrix products  54.7 us (6%)
  blocking collectives  48.2 us (5%)
  starting transfers between devices  20 us (2%)
  waiting for transfers between devices  13.4 us (1%)
    gather x768, local copies, waits for them, and re-layouts  661 us
    another operation x4, other arithmetic, fit_coefficients(): factor = jnp.linalg.cholesky(gram_total)  41.2 us
    psum x1, blocking collectives, fit_coefficients(): gram_total, right_total = lax.psum((gram_total, right_total), 'patch')  41 us
    another operation x3, other arithmetic, fit_coefficients(): jax.scipy.linalg.cho_solve((factor, True), right_total[..., None])[..., 0]  34.6 us
    reduce_sum x24, other arithmetic, model_block(): model = model + jnp.sum(weighted, axis=1)  31.6 us
    concatenate x136, local copies, waits for them, and re-layouts, fit_block(): images = jnp.concatenate(pieces_list, axis=1)  22.8 us
    dot_general x16, matrix products, filtered_block(): jnp.einsum('ry,nyx->nrx', row_matrix, windows, preferred_element_type=jnp...  20 us
  transfers between devices with their start and end apart: 4, of which 2 were waited for; matrix products, arithmetic and copies ran while one was open for 68% of the time, Pallas kernels for 0%

commit v1 on v0

v1 whole, which is shorter than its diff:
```python
import functools

import jax
import jax.numpy as jnp
import numpy as np
from jax import lax
from jax.experimental import pallas as pl
from jax.experimental.pallas import tpu as pltpu
from jax.sharding import PartitionSpec as P

KR = 10
NF = 11
NB = 28
VIS_DEV = 16
ROWS = 32
RHS = NB
GROUP = 8
LANES = 128
VMEM_BYTES = 60 * 1024 * 1024


gauss_widths = (1.0, 2.0, 4.0)
poly_degrees = (4, 2, 2)


def filter_table(radius):
    tap_points = np.arange(-radius, radius + 1) * 1.0
    raw_columns = []
    for width_value, degree in zip(gauss_widths, poly_degrees):
        bell_curve = np.exp(-tap_points * tap_points / (2.0 * width_value * width_value))
        for power_index in range(degree + 1):
            raw_columns.append(bell_curve * (tap_points / radius) ** power_index)
    orthonormal = []
    for column in raw_columns:
        vector = column.copy()
        for repeat_index in range(2):
            for earlier in orthonormal:
                vector = vector - np.dot(earlier, vector) * earlier
        orthonormal.append(vector / np.sqrt(np.dot(vector, vector)))
    return np.stack(orthonormal, axis=1).astype(np.float32)


def pair_layout():
    column_ids = []
    row_ids = []
    filter_runs = []
    offset = 0
    for degree in poly_degrees:
        for first_index in range(degree + 1):
            filter_runs.append((offset + first_index, offset, offset + degree - first_index + 1))
            for second_index in range(degree + 1 - first_index):
                column_ids.append(offset + first_index)
                row_ids.append(offset + second_index)
        offset += degree + 1
    return (column_ids, row_ids, filter_runs)


def band_tables(start_rows, patch_rows):
    values = filter_table(KR)
    taps_count = 2 * KR + 1
    row_band = np.zeros((NF, start_rows, patch_rows), np.float32)
    for start in range(start_rows):
        stop = min(start + taps_count, patch_rows)
        row_band[:, start, start:stop] = values.T[:, : stop - start]
    column_band = np.zeros((2 * LANES, NF, LANES), np.float32)
    for out_column in range(LANES):
        column_band[out_column : out_column + taps_count, :, out_column] = values
    return (
        jnp.asarray(row_band.astype(jnp.bfloat16)),
        jnp.asarray(column_band.reshape(2 * LANES, NF * LANES).astype(jnp.bfloat16)),
    )


def basis_runs():
    column_ids, row_ids, _ = pair_layout()
    index_of = {pair: k for k, pair in enumerate(zip(column_ids, row_ids))}
    runs = []
    offset = 0
    for degree in poly_degrees:
        for second in range(degree + 1):
            b = offset + second
            count = degree + 1 - second
            runs.append((b, offset, [index_of[(offset + i, b)] for i in range(count)]))
        offset += degree + 1
    return runs


def chunk_rows(group, per_tile):
    return -(-group * per_tile // 16) * 16


def peers_signal(barrier, axis, me, count):
    def one(i, carry):
        pl.semaphore_signal(
            barrier,
            inc=1,
            device_id={axis: lax.rem(me + 1 + i, count)},
            device_id_type=pl.DeviceIdType.MESH,
        )
        return carry

    lax.fori_loop(0, count - 1, one, 0)


def push(source, target, send_sem, recv_sem, axis, peer):
    return pltpu.make_async_remote_copy(
        src_ref=source,
        dst_ref=target,
        send_sem=send_sem,
        recv_sem=recv_sem,
        device_id={axis: peer},
        device_id_type=pl.DeviceIdType.MESH,
    )


def dispatch_kernel(
    patches,
    visit_parts,
    capacity,
    source_ref,
    live_ref,
    template_ref,
    science_ref,
    sigma_ref,
    details_ref,
    whole_ref,
    arrived_ref,
    arrived_details_ref,
    stage,
    packed,
    template_send,
    template_recv,
    tile_send,
    tile_recv,
    details_send,
    details_recv,
):
    me = lax.axis_index("patch")
    my_visit = lax.axis_index("visit")
    group = min(GROUP, capacity)
    chunk = chunk_rows(group, 4)
    peer_rows = capacity // group * chunk
    share = template_ref.shape[0]

    barrier = pltpu.get_barrier_semaphore()
    peers_signal(barrier, "patch", me, patches)
    peers_signal(barrier, "visit", my_visit, visit_parts)
    if chunk != 4 * group:
        stage[...] = jnp.zeros_like(stage)

    def template_rows(index):
        return whole_ref.at[pl.ds(pl.multiple_of(index * share, 16), share), :]

    def tile_rows(ref, index):
        return ref.at[pl.ds(pl.multiple_of(index * peer_rows, 16), peer_rows), :]

    template_rows(my_visit)[...] = template_ref[...].astype(jnp.bfloat16)
    arrived_details_ref[me] = details_ref[me]
    pl.semaphore_wait(barrier, patches - 1 + visit_parts - 1)

    def template_copy(peer, owner):
        return push(
            template_rows(owner),
            template_rows(owner),
            template_send.at[peer],
            template_recv.at[owner],
            "visit",
            peer,
        )

    def details_copy(peer, owner):
        return push(
            details_ref.at[peer],
            arrived_details_ref.at[owner],
            details_send.at[peer],
            details_recv.at[owner],
            "patch",
            peer,
        )

    def tile_copy(peer, owner):
        return push(
            tile_rows(packed, peer),
            tile_rows(arrived_ref, owner),
            tile_send.at[peer],
            tile_recv.at[owner],
            "patch",
            peer,
        )

    for i in range(1, visit_parts):
        template_copy(lax.rem(my_visit + i, visit_parts), my_visit).start()

    def pack(peer):
        def pack_group(q, carry):
            base = pl.multiple_of(peer * peer_rows + q * chunk, 16)
            for t in range(group):
                slot = peer * capacity + q * group + t
                tile = source_ref[slot]
                sigma = sigma_ref[tile] * live_ref[slot]
                stage[pl.ds(base + 4 * t, 2), :] = science_ref[tile] * sigma
                stage[pl.ds(base + 4 * t + 2, 2), :] = sigma
            return carry

        lax.fori_loop(0, capacity // group, pack_group, 0)
        rows = pl.ds(pl.multiple_of(peer * peer_rows, 16), peer_rows)
        return rows, stage[rows, :].astype(jnp.bfloat16)

    def pack_and_send(i, carry):
        peer = lax.rem(me + 1 + i, patches)
        details_copy(peer, me).start()
        rows, values = pack(peer)
        packed[rows, :] = values
        tile_copy(peer, me).start()
        return carry

    lax.fori_loop(0, patches - 1, pack_and_send, 0)
    rows, values = pack(me)
    arrived_ref[rows, :] = values

    for i in range(1, visit_parts):
        peer = lax.rem(my_visit + i, visit_parts)
        template_copy(peer, my_visit).wait_send()
        template_copy(peer, peer).wait_recv()

    def finish(i, carry):
        peer = lax.rem(me + 1 + i, patches)
        details_copy(peer, me).wait_send()
        tile_copy(peer, me).wait_send()
        details_copy(peer, peer).wait_recv()
        tile_copy(peer, peer).wait_recv()
        return carry

    lax.fori_loop(0, patches - 1, finish, 0)


def fit_kernel(
    capacity,
    visit_ref,
    row_ref,
    column_ref,
    template_ref,
    row_band_ref,
    column_band_ref,
    arrived_ref,
    gram_ref,
    picked_out,
    filtered,
    images,
    total,
    picked_all,
    picked_sems,
):
    start_rows = row_band_ref.shape[1]
    image_rows = images.shape[1] // ROWS
    patch_columns = template_ref.shape[1]
    blocks = patch_columns // LANES
    slot_count = picked_all.shape[0]
    group = min(GROUP, capacity)
    chunk = chunk_rows(group, 4)

    for b in range(NF):
        filtered[b, :, :patch_columns] = jnp.dot(
            row_band_ref[b], template_ref[...], preferred_element_type=jnp.float32
        ).astype(jnp.bfloat16)
        filtered[b, :, patch_columns:] = jnp.zeros((start_rows, LANES), jnp.bfloat16)

    def column_block(j, carry):
        at = pl.multiple_of(j * LANES, LANES)
        for b, first, indices in basis_runs():
            product = jnp.dot(
                filtered[b, :, pl.ds(at, 2 * LANES)],
                column_band_ref[:, first * LANES : (first + len(indices)) * LANES],
                preferred_element_type=jnp.float32,
            )
            for i, k in enumerate(indices):
                images[j, k * image_rows : k * image_rows + start_rows, :] = product[
                    :, i * LANES : (i + 1) * LANES
                ]
        return carry

    lax.fori_loop(0, blocks, column_block, 0)

    total[...] = jnp.zeros_like(total)
    lane = lax.broadcasted_iota(jnp.int32, (8, LANES), 1)
    eighth = lax.broadcasted_iota(jnp.int32, (8, LANES), 0)
    basis = lax.broadcasted_iota(jnp.int32, (ROWS, LANES), 0)
    part = lax.broadcasted_iota(jnp.int32, (ROWS, LANES), 1) // ROWS

    def pick(slot):
        column = column_ref[slot]
        block = column // LANES
        shift = column % LANES
        halves = []
        for i in range(2):
            pieces = []
            for k in range(0, ROWS, 8):
                rows = pl.ds(k * image_rows + row_ref[slot] + i, 8, stride=image_rows)
                piece = pltpu.roll(
                    jnp.where(lane >= shift, images[block, rows, :], images[block + 1, rows, :]),
                    (LANES - shift) % LANES,
                    axis=1,
                )
                if k + 8 >= NB:
                    constant = jnp.where(eighth + k == NB - 1, 1.0, 0.0)
                    piece = jnp.where(eighth + k < NB - 1, piece, constant)
                pieces.append(piece)
            halves.append(jnp.concatenate(pieces, axis=0))
        return halves

    def tile_group(g, carry):
        chunks = [
            arrived_ref[pl.ds(pl.multiple_of((g * (GROUP // group) + c) * chunk, 16), chunk), :]
            for c in range(GROUP // group)
        ]
        chunks = [values.astype(jnp.float32) for values in chunks]
        designs = []
        for t in range(GROUP):
            s = g * GROUP + t
            values = chunks[t // group][t % group * 4 : t % group * 4 + 4]
            halves = pick(s)
            for i in range(2):
                picked_all[s, i * ROWS : (i + 1) * ROWS, :] = halves[i]
            designs.append(
                jnp.concatenate(
                    [
                        jnp.where(
                            basis == RHS,
                            values[i : i + 1],
                            halves[i] * values[2 + i : 3 + i],
                        ).astype(jnp.bfloat16)
                        for i in range(2)
                    ],
                    axis=1,
                )
            )
        design = jnp.concatenate(designs, axis=0)
        products = lax.dot_general(
            design, design, (((1,), (1,)), ((), ())), preferred_element_type=jnp.float32
        )
        per = LANES // ROWS
        for t in range(GROUP):
            own = products[
                t * ROWS : (t + 1) * ROWS, (t // per) * LANES : (t // per + 1) * LANES
            ]
            total[visit_ref[g * GROUP + t]] += jnp.where(part == t % per, own, 0.0)
        return carry

    stages = picked_sems.shape[0]
    groups = slot_count // GROUP // stages
    copies = []
    for n in range(stages):
        lax.fori_loop(n * groups, (n + 1) * groups, tile_group, 0)
        rows = pl.ds(n * groups * GROUP, groups * GROUP)
        copies.append(
            pltpu.make_async_copy(picked_all.at[rows], picked_out.at[rows], picked_sems.at[n])
        )
        copies[-1].start()

    owners = gram_ref.shape[0]
    per_owner = VIS_DEV // owners
    for owner in range(owners):
        merged = jnp.zeros((ROWS, LANES), jnp.float32)
        for i in range(per_owner):
            folded = total[owner * per_owner + i]
            folded = folded + pltpu.roll(folded, 2 * ROWS, axis=1)
            folded = folded + pltpu.roll(folded, ROWS, axis=1)
            merged = jnp.where(part == i, folded, merged)
        gram_ref[owner] = merged
    for copy in copies:
        copy.wait()


def solve_systems(system):
    row_id = lax.broadcasted_iota(jnp.int32, system.shape, 1)
    column_id = lax.broadcasted_iota(jnp.int32, system.shape, 2)
    for p in range(NB):
        pivot_row = system[:, p : p + 1, :]
        inverse = 1.0 / system[:, p : p + 1, p : p + 1]
        factor = system[:, :, p : p + 1] * inverse
        system = jnp.where(row_id == p, system, system - factor * pivot_row)
    diagonal = jnp.sum(jnp.where(row_id == column_id, system, 0.0), axis=2, keepdims=True)
    solved = system[:, :, RHS : RHS + 1] / diagonal
    return jnp.where(row_id < NB, jnp.broadcast_to(solved, system.shape), 0.0)


def finish_kernel(
    patches,
    capacity,
    visit_ref,
    place_ref,
    gram_ref,
    picked_in,
    science_ref,
    difference_ref,
    coefficient_ref,
    picked,
    grams,
    solved,
    arrived_solved,
    stage,
    packed,
    returned,
    returned_wide,
    picked_sem,
    gram_send,
    gram_recv,
    solved_send,
    solved_recv,
    model_send,
    model_recv,
):
    me = lax.axis_index("patch")
    owners = gram_ref.shape[0]
    per_owner = VIS_DEV // owners
    group = min(GROUP, capacity)
    chunk = chunk_rows(group, 2)
    peer_rows = capacity // group * chunk
    load = pltpu.make_async_copy(picked_in, picked, picked_sem)
    load.start()
    barrier = pltpu.get_barrier_semaphore()
    peers_signal(barrier, "patch", me, patches)
    if chunk != 2 * group:
        stage[...] = jnp.zeros_like(stage)
    pl.semaphore_wait(barrier, patches - 1)

    def when_owner(index, action):
        if owners == patches:
            action()
        else:
            pl.when(index < owners)(action)

    def each_peer(action):
        def one(i, carry):
            action(lax.rem(me + 1 + i, patches))
            return carry

        lax.fori_loop(0, patches - 1, one, 0)

    def gram_copy(peer, sender):
        return push(
            gram_ref.at[peer], grams.at[sender], gram_send.at[peer], gram_recv.at[sender],
            "patch", peer,
        )

    def solved_copy(peer, sender):
        return push(
            solved, arrived_solved.at[sender], solved_send.at[peer], solved_recv.at[sender],
            "patch", peer,
        )

    def tile_rows(ref, index):
        return ref.at[pl.ds(pl.multiple_of(index * peer_rows, 16), peer_rows), :]

    def model_copy(peer, sender):
        return push(
            tile_rows(packed, peer), tile_rows(returned, sender), model_send.at[peer],
            model_recv.at[sender], "patch", peer,
        )

    each_peer(lambda peer: when_owner(peer, lambda: gram_copy(peer, me).start()))

    def solve_own():
        grams[me] = gram_ref[me]
        each_peer(lambda peer: gram_copy(lax.rem(me, owners), peer).wait_recv())
        summed = jnp.sum(grams[...], axis=0)
        systems = [summed] + [
            pltpu.roll(summed, LANES - i * ROWS, axis=1) for i in range(1, per_owner)
        ]
        values = solve_systems(jnp.stack(systems, axis=0))
        lane = lax.broadcasted_iota(jnp.int32, (ROWS, LANES), 1)
        merged = values[0]
        for i in range(1, per_owner):
            merged = jnp.where(lane == i, values[i], merged)
        solved[...] = merged
        arrived_solved[me] = merged
        each_peer(lambda peer: solved_copy(peer, me).start())

    when_owner(me, solve_own)
    each_peer(
        lambda peer: when_owner(peer, lambda: solved_copy(peer, peer).wait_recv())
    )
    for v in range(VIS_DEV):
        i = v % per_owner
        coefficient_ref[v] = jnp.broadcast_to(
            arrived_solved[v // per_owner][:, i : i + 1], (ROWS, LANES)
        )
    load.wait()

    def model_of(peer):
        def model_group(q, carry):
            base = pl.multiple_of(peer * peer_rows + q * chunk, 16)
            for t in range(group):
                s = peer * capacity + q * group + t
                values = coefficient_ref[visit_ref[s]]
                for i in range(2):
                    stage[pl.ds(base + 2 * t + i, 1), :] = jnp.sum(
                        picked[s, i * ROWS : (i + 1) * ROWS, :] * values, axis=0, keepdims=True
                    )
            return carry

        lax.fori_loop(0, capacity // group, model_group, 0)
        rows = pl.ds(pl.multiple_of(peer * peer_rows, 16), peer_rows)
        return rows, stage[rows, :].astype(jnp.bfloat16)

    def model_and_send(peer):
        rows, values = model_of(peer)
        packed[rows, :] = values
        model_copy(peer, me).start()

    each_peer(model_and_send)
    rows, values = model_of(me)
    returned[rows, :] = values

    def finish(peer):
        when_owner(peer, lambda: gram_copy(peer, me).wait_send())
        when_owner(me, lambda: solved_copy(peer, me).wait_send())
        model_copy(peer, me).wait_send()
        model_copy(peer, peer).wait_recv()

    each_peer(finish)
    returned_wide[...] = returned[...].astype(jnp.float32)

    def subtract(q, carry):
        for t in range(GROUP):
            tile = q * GROUP + t
            difference_ref[tile] = science_ref[tile] - returned_wide[pl.ds(place_ref[tile], 2), :]
        return carry

    lax.fori_loop(0, science_ref.shape[0] // GROUP, subtract, 0)


def per_device(science, inverse_sigma, template, destination, offsets, visit_local):
    patches = lax.axis_size("patch")
    visit_parts = lax.axis_size("visit")
    tile_count, row_count, column_count = science.shape
    capacity = max(2, 2 * tile_count // patches)
    slot_count = patches * capacity
    patch_rows, patch_columns = template.shape[1] * visit_parts, template.shape[2]
    start_rows = -(-(patch_rows - 2 * KR) // 16) * 16
    image_rows = start_rows + 8
    row_band, column_band = band_tables(start_rows, patch_rows)
    order_ids = jnp.arange(tile_count, dtype=jnp.int32)
    same_patch = destination[:, None] == destination[None, :]
    before = order_ids[None, :] < order_ids[:, None]
    tile_rank = jnp.sum(jnp.where(same_patch & before, 1, 0), axis=1).astype(jnp.int32)
    slot_of_tile = destination * capacity + tile_rank
    slot_ids = jnp.arange(slot_count, dtype=jnp.int32)
    holds = slot_of_tile[None, :] == slot_ids[:, None]
    routed = jnp.stack(
        [jnp.ones_like(order_ids), order_ids, visit_local, offsets[:, 0], offsets[:, 1]], axis=0
    )
    routed = jnp.sum(jnp.where(holds[None], routed[:, None, :], 0), axis=2)
    details = jnp.pad(
        routed[2:].reshape(3, patches, capacity).transpose(1, 0, 2),
        ((0, 0), (0, 5), (0, LANES - capacity)),
    )
    group = min(GROUP, capacity)
    tile_chunk = chunk_rows(group, 4)
    tile_total = slot_count // group * tile_chunk
    model_chunk = chunk_rows(group, 2)
    model_total = slot_count // group * model_chunk
    place_of_tile = slot_of_tile // group * model_chunk + slot_of_tile % group * 2

    smem = pl.BlockSpec(memory_space=pltpu.SMEM)
    vmem = pl.BlockSpec(memory_space=pltpu.VMEM)
    anywhere = pl.BlockSpec(memory_space=pl.ANY)
    dma = pltpu.SemaphoreType.DMA
    whole_template, arrived, arrived_details = pl.pallas_call(
        functools.partial(dispatch_kernel, patches, visit_parts, capacity),
        out_shape=(
            jax.ShapeDtypeStruct((patch_rows, patch_columns), jnp.bfloat16),
            jax.ShapeDtypeStruct((tile_total, LANES), jnp.bfloat16),
            jax.ShapeDtypeStruct((patches, 8, LANES), jnp.int32),
        ),
        in_specs=[smem] * 2 + [vmem] * 4,
        out_specs=(vmem,) * 3,
        scratch_shapes=[
            pltpu.VMEM((tile_total, LANES), jnp.float32),
            pltpu.VMEM((tile_total, LANES), jnp.bfloat16),
            dma((visit_parts,)),
            dma((visit_parts,)),
        ]
        + [dma((patches,))] * 4,
        compiler_params=pltpu.CompilerParams(
            vmem_limit_bytes=VMEM_BYTES, collective_id=0, has_side_effects=True
        ),
    )(
        routed[1],
        routed[0].astype(jnp.float32),
        template[0],
        science,
        inverse_sigma,
        details,
    )
    arrived_details = arrived_details[:, :3, :capacity].transpose(1, 0, 2).reshape(3, slot_count)
    visits = arrived_details[0]
    owners = min(patches, VIS_DEV)
    picked_shape = (slot_count, row_count * ROWS, LANES)
    gram, picked = pl.pallas_call(
        functools.partial(fit_kernel, capacity),
        out_shape=(
            jax.ShapeDtypeStruct((owners, ROWS, LANES), jnp.float32),
            jax.ShapeDtypeStruct(picked_shape, jnp.float32),
        ),
        in_specs=[smem] * 3 + [vmem] * 4,
        out_specs=(vmem, anywhere),
        scratch_shapes=[
            pltpu.VMEM((NF, start_rows, patch_columns + LANES), jnp.bfloat16),
            pltpu.VMEM((patch_columns // LANES, image_rows * ROWS, LANES), jnp.float32),
            pltpu.VMEM((VIS_DEV, ROWS, LANES), jnp.float32),
            pltpu.VMEM(picked_shape, jnp.float32),
            dma((4,)),
        ],
        compiler_params=pltpu.CompilerParams(vmem_limit_bytes=VMEM_BYTES),
    )(
        visits,
        arrived_details[1],
        arrived_details[2],
        whole_template,
        row_band,
        column_band,
        arrived,
    )
    difference, solved = pl.pallas_call(
        functools.partial(finish_kernel, patches, capacity),
        out_shape=(
            jax.ShapeDtypeStruct(science.shape, jnp.float32),
            jax.ShapeDtypeStruct((VIS_DEV, ROWS, LANES), jnp.float32),
        ),
        in_specs=[smem] * 2 + [vmem, anywhere, vmem],
        out_specs=(vmem, vmem),
        scratch_shapes=[
            pltpu.VMEM(picked_shape, jnp.float32),
            pltpu.VMEM((patches, ROWS, LANES), jnp.float32),
            pltpu.VMEM((ROWS, LANES), jnp.float32),
            pltpu.VMEM((owners, ROWS, LANES), jnp.float32),
            pltpu.VMEM((model_total, LANES), jnp.float32),
            pltpu.VMEM((model_total, LANES), jnp.bfloat16),
            pltpu.VMEM((model_total, LANES), jnp.bfloat16),
            pltpu.VMEM((model_total, LANES), jnp.float32),
            dma,
            dma((owners,)),
            dma((patches,)),
            dma((patches,)),
            dma((owners,)),
            dma((patches,)),
            dma((patches,)),
        ],
        compiler_params=pltpu.CompilerParams(
            vmem_limit_bytes=VMEM_BYTES, collective_id=1, has_side_effects=True
        ),
    )(visits, place_of_tile, gram, picked, science)
    return (difference, solved[:, :NB, 0])


def solution(mesh):
    return jax.shard_map(
        per_device,
        mesh=mesh,
        in_specs=(
            P(("patch", "visit"), None, None),
            P(("patch", "visit"), None, None),
            P("patch", "visit", None),
            P(("patch", "visit")),
            P(("patch", "visit"), None),
            P(("patch", "visit")),
        ),
        out_specs=(P(("patch", "visit"), None, None), P("visit", None)),
        check_vma=False,
    )
```

time: 980 us -> 73.1 us (0.07)
  local copies, waits for them, and re-layouts: 711 us -> 8.11 us
  other arithmetic: 123 us -> 3 us
  Pallas kernels: 0 us -> 60.9 us
  matrix products: 54.7 us -> 0 us
  blocking collectives: 48.2 us -> 0 us
  starting transfers between devices: 20 us -> 0 us
  waiting for transfers between devices: 13.4 us -> 0 us
    gather x790 -> x0, local copies, waits for them, and re-layouts: 680 us -> none
    another operation x7 -> x0, other arithmetic: 75.8 us -> none  [the longest x4 41.2 us: fit_coefficients(): factor = jnp.linalg.cholesky(gram_total)]
    pallas_call x0 -> x3, Pallas kernels: none -> 60.9 us  [the longest x1 23.1 us: per_device(): pl.pallas_call(functools.partial(fit_kernel, capacity), out_shape=(jax.Sh...]
    dot_general x144 -> x0, matrix products: 53.8 us -> none  [the longest x16 20 us: filtered_block(): jnp.einsum('ry,nyx->nrx', row_matrix, windows, preferred_element_type=jnp...]
    psum x1 -> x0, blocking collectives: 41 us -> none  [fit_coefficients(): gram_total, right_total = lax.psum((gram_total, right_total), 'patch')]
    reduce_sum x27 -> x1, other arithmetic: 33.4 us -> 0.24 us  [per_device(): routed = jnp.sum(jnp.where(holds[None], routed[:, None, :], 0), axis=2)]
    concatenate x144 -> x0, local copies, waits for them, and re-layouts: 22.9 us -> none  [the longest x136 22.8 us: fit_block(): images = jnp.concatenate(pieces_list, axis=1)]
    all_to_all x4 -> x0, starting transfers between devices: 20 us -> none  [the longest x1 7.28 us: per_device(): lax.all_to_all(details.reshape(patches, capacity, 4), 'patch', split_axis...]
  transfers between devices with their start and end apart: 4 -> 0, of which waited for: 2 -> 0; matrix products, arithmetic and copies ran while one was open for 68% -> 0% of each run, Pallas kernels for 0% -> 0%
where the time goes in v1:
time: 73.1 us; the launch traced here: 72.7 us
  Pallas kernels  60.9 us (83%)
  local copies, waits for them, and re-layouts  8.11 us (11%)
  other arithmetic  3 us (4%)
    pallas_call x1, Pallas kernels, per_device(): pl.pallas_call(functools.partial(fit_kernel, capacity), out_shape=(jax.Sh...  23.1 us
    pallas_call x1, Pallas kernels, per_device(): pl.pallas_call(functools.partial(finish_kernel, patches, capacity), out_s...  23.1 us
    pallas_call x1, Pallas kernels, per_device(): pl.pallas_call(functools.partial(dispatch_kernel, patches, visit_parts, c...  14.6 us
    slice x1, local copies, waits for them, and re-layouts, per_device(): return (difference, solved[:, :NB, 0])  1.69 us
    unnamed x1, local copies, waits for them, and re-layouts  1.57 us

profile of v1, /device:TPU:0, one launch (start us, length us, event | category | flops | bytes accessed | tf_op | source)
XLA Modules:
  0.0 72.7 jit_solution(15524903241155515724)
XLA Ops:
  0.6 0.9 %select_reduce_fusion.1 = s32[128]{0:T(128)S(1)} fusion(s32[128]{0:T(128)} %param.11), kind=kLoop, calls=%fused_computation.3 | loop fusion | flops 81792 | bytes 1024 | tf_op jit(solution)/shard_map/reduce_sum | solution.py:546
  1.5 1.3 %fusion.2 = (s32[128]{0:T(128)}, s32[128]{0:T(128)S(1)}) fusion(s32[128]{0:T(128)S(1)} %select_reduce_fusion.1, s32[128]{0:T(128)} %param.11), kind=kLoop, calls=%fused_computation.18 | loop fusion | flops 3072 | bytes 2048 | tf_op jit(solution)/shard_map/add | solution.py:563
  2.8 0.8 %slice_bitcast_fusion.1 = (s32[1,128]{1,0:T(1,128)S(1)}, s32[1,128]{1,0:T(1,128)S(1)}) fusion(s32[128,2]{0,1:T(2,128)} %param.12), kind=kLoop, calls=%fused_computation.19 | loop fusion | bytes 2048 | tf_op jit(solution)/shard_map/stack;squeeze | solution.py:550
  3.6 0.7 stack.8
  4.3 0.2 select_reduce_fusion
  4.5 0.6 slice_convert_fusion
  5.1 0.1 reshape.39
  5.2 0.6 pad.4.details_ref
  5.8 14.6 %shard_map.95 = (bf16[256,1024]{1,0:T(8,128)(2,1)}, bf16[1024,128]{1,0:T(8,128)(2,1)}, s32[8,8,128]{2,1,0:T(8,128)}) custom-call(s32[256]{0:T(256)} %bitcast.16, f32[256]{0:T(256)} %bitcast.15, f32[64,1024]{1,0:T(8,128)} %bitcast.13, f32[128,2,128]{2,1,0:T(2,128)} %science_ref.3, f32[128,2,128]{2,1,0:T(2,128)} %sigma_ref.1, s32[8,8,128]{2,1,0:T(8,128)} %pad.4.details_ref), custom_call_target="tpu_custom_call" | custom-call | tf_op jit(solution)/shard_map/pallas_call | solution.py:569
  20.5 0.8 %slice_bitcast_fusion = s32[3,8,32]{2,0,1:T(4,128)S(1)} fusion(s32[8,8,128]{2,1,0:T(8,128)} %get-tuple-element.9), kind=kLoop, calls=%fused_computation.7 | loop fusion | bytes 6144 | tf_op jit(solution)/shard_map/transpose | solution.py:596
  21.3 0.6 squeeze.23.column_ref
  21.9 0.6 squeeze.21.visit_ref
  22.5 0.6 squeeze.22.row_ref
  23.2 23.1 %shard_map.96 = (f32[8,32,128]{2,1,0:T(8,128)}, f32[256,64,128]{2,1,0:T(8,128)}) custom-call(s32[256]{0:T(256)} %squeeze.21.visit_ref, s32[256]{0:T(256)} %squeeze.22.row_ref, s32[256]{0:T(256)} %squeeze.23.column_ref, bf16[256,1024]{1,0:T(8,128)(2,1)} %get-tuple-element.10.template_ref, bf16[11,240,256]{2,1,0:T(8,128)(2,1)} %constant.41.clone.row_band_ref, ...), custom_call_target="tpu_custom_call" | custom-call | tf_op jit(solution)/shard_map/pallas_call | solution.py:600
  46.3 23.1 %shard_map.97 = (f32[128,2,128]{2,1,0:T(2,128)}, f32[16,32,128]{2,1,0:T(8,128)}) custom-call(s32[256]{0:T(256)} %squeeze.21.visit_ref, s32[128]{0:T(128)} %get-tuple-element.19.place_ref, f32[8,32,128]{2,1,0:T(8,128)} %get-tuple-element.12.gram_ref, f32[256,64,128]{2,1,0:T(8,128)} %get-tuple-element.13.picked_in, f32[128,2,128]{2,1,0:T(2,128)} %science_ref.3), custom_call_target="tpu_custom_call" | custom-call | tf_op jit(solution)/shard_map/pallas_call | solution.py:625
  69.4 1.7 %slice_reduce_fusion = f32[16,28]{1,0:T(8,128)} fusion(f32[16,32,128]{2,1,0:T(8,128)} %get-tuple-element.15), kind=kLoop, calls=%fused_computation.1 | loop fusion | bytes 3584 | tf_op jit(solution)/shard_map/slice | solution.py:654
  71.1 1.6 %copy.15 = f32[128,2,128]{2,1,0:T(2,128)} copy(f32[128,2,128]{2,1,0:T(2,128)} %get-tuple-element.27) | data formatting | bytes 262144
  (6 shorter events, 0.1 us)

commit v2 on v1

v2 whole, which is shorter than its diff:
```python
import functools

import jax
import jax.numpy as jnp
import numpy as np
from jax import lax
from jax.experimental import pallas as pl
from jax.experimental.pallas import tpu as pltpu
from jax.sharding import PartitionSpec as P

KR = 10
NF = 11
NB = 28
VIS_DEV = 16
ROWS = 32
RHS = NB
GROUP = 8
LANES = 128
VMEM_BYTES = 60 * 1024 * 1024


gauss_widths = (1.0, 2.0, 4.0)
poly_degrees = (4, 2, 2)


def filter_table(radius):
    tap_points = np.arange(-radius, radius + 1) * 1.0
    raw_columns = []
    for width_value, degree in zip(gauss_widths, poly_degrees):
        bell_curve = np.exp(-tap_points * tap_points / (2.0 * width_value * width_value))
        for power_index in range(degree + 1):
            raw_columns.append(bell_curve * (tap_points / radius) ** power_index)
    orthonormal = []
    for column in raw_columns:
        vector = column.copy()
        for repeat_index in range(2):
            for earlier in orthonormal:
                vector = vector - np.dot(earlier, vector) * earlier
        orthonormal.append(vector / np.sqrt(np.dot(vector, vector)))
    return np.stack(orthonormal, axis=1).astype(np.float32)


def pair_layout():
    column_ids = []
    row_ids = []
    filter_runs = []
    offset = 0
    for degree in poly_degrees:
        for first_index in range(degree + 1):
            filter_runs.append((offset + first_index, offset, offset + degree - first_index + 1))
            for second_index in range(degree + 1 - first_index):
                column_ids.append(offset + first_index)
                row_ids.append(offset + second_index)
        offset += degree + 1
    return (column_ids, row_ids, filter_runs)


def band_tables(start_rows, patch_rows):
    values = filter_table(KR)
    taps_count = 2 * KR + 1
    row_band = np.zeros((NF, start_rows, patch_rows), np.float32)
    for start in range(start_rows):
        stop = min(start + taps_count, patch_rows)
        row_band[:, start, start:stop] = values.T[:, : stop - start]
    column_band = np.zeros((2 * LANES, NF, LANES), np.float32)
    for out_column in range(LANES):
        column_band[out_column : out_column + taps_count, :, out_column] = values
    return (
        jnp.asarray(row_band.astype(jnp.bfloat16)),
        jnp.asarray(column_band.reshape(2 * LANES, NF * LANES).astype(jnp.bfloat16)),
    )


def basis_runs():
    column_ids, row_ids, _ = pair_layout()
    index_of = {pair: k for k, pair in enumerate(zip(column_ids, row_ids))}
    runs = []
    offset = 0
    for degree in poly_degrees:
        for second in range(degree + 1):
            b = offset + second
            count = degree + 1 - second
            runs.append((b, offset, [index_of[(offset + i, b)] for i in range(count)]))
        offset += degree + 1
    return runs


def chunk_rows(group, per_tile):
    return -(-group * per_tile // 16) * 16


def peers_signal(barrier, axis, me, count):
    def one(i, carry):
        pl.semaphore_signal(
            barrier,
            inc=1,
            device_id={axis: lax.rem(me + 1 + i, count)},
            device_id_type=pl.DeviceIdType.MESH,
        )
        return carry

    lax.fori_loop(0, count - 1, one, 0)


def push(source, target, send_sem, recv_sem, axis, peer):
    return pltpu.make_async_remote_copy(
        src_ref=source,
        dst_ref=target,
        send_sem=send_sem,
        recv_sem=recv_sem,
        device_id={axis: peer},
        device_id_type=pl.DeviceIdType.MESH,
    )


def solve_systems(system):
    row_id = lax.broadcasted_iota(jnp.int32, system.shape, 1)
    column_id = lax.broadcasted_iota(jnp.int32, system.shape, 2)
    for p in range(NB):
        pivot_row = system[:, p : p + 1, :]
        inverse = 1.0 / system[:, p : p + 1, p : p + 1]
        factor = system[:, :, p : p + 1] * inverse
        system = jnp.where(row_id == p, system, system - factor * pivot_row)
    diagonal = jnp.sum(jnp.where(row_id == column_id, system, 0.0), axis=2, keepdims=True)
    solved = system[:, :, RHS : RHS + 1] / diagonal
    return jnp.where(row_id < NB, jnp.broadcast_to(solved, system.shape), 0.0)


def image_kernel(
    patches,
    visit_parts,
    capacity,
    place_ref,
    template_ref,
    science_ref,
    sigma_ref,
    details_ref,
    row_band_ref,
    column_band_ref,
    model_ref,
    coefficient_ref,
    whole,
    arrived,
    arrived_details,
    routes,
    stage,
    packed,
    filtered,
    images,
    picked,
    running,
    gram,
    grams,
    solved,
    arrived_solved,
    spread,
    model_packed,
    returned,
    routes_sem,
    template_send,
    template_recv,
    tile_send,
    tile_recv,
    details_send,
    details_recv,
    gram_send,
    gram_recv,
    solved_send,
    solved_recv,
    model_send,
    model_recv,
):
    me = lax.axis_index("patch")
    my_visit = lax.axis_index("visit")
    slot_count = patches * capacity
    group = min(GROUP, capacity)
    tile_chunk = chunk_rows(group, 4)
    tile_peer = capacity // group * tile_chunk
    model_chunk = chunk_rows(group, 2)
    model_peer = capacity // group * model_chunk
    share, patch_columns = template_ref.shape
    start_rows = row_band_ref.shape[1]
    image_rows = images.shape[1] // ROWS
    owners = gram.shape[0]
    per_owner = VIS_DEV // owners

    def rows_of(index, count):
        return pl.ds(pl.multiple_of(index * count, 16), count)

    def each_peer(action):
        def one(i, carry):
            action(lax.rem(me + 1 + i, patches))
            return carry

        lax.fori_loop(0, patches - 1, one, 0)

    def when_owner(index, action):
        if owners == patches:
            action()
        else:
            pl.when(index < owners)(action)

    def template_copy(peer, owner):
        rows = whole.at[rows_of(owner, share), :]
        return push(rows, rows, template_send.at[peer], template_recv.at[owner], "visit", peer)

    def patch_copy(source, target, send, recv, peer, sender):
        return push(source, target, send.at[peer], recv.at[sender], "patch", peer)

    def details_copy(peer, sender):
        return patch_copy(
            details_ref.at[peer], arrived_details.at[sender], details_send, details_recv, peer, sender
        )

    def tile_copy(peer, sender):
        return patch_copy(
            packed.at[rows_of(peer, tile_peer), :],
            arrived.at[rows_of(sender, tile_peer), :],
            tile_send,
            tile_recv,
            peer,
            sender,
        )

    def gram_copy(peer, sender):
        return patch_copy(gram.at[peer], grams.at[sender], gram_send, gram_recv, peer, sender)

    def solved_copy(peer, sender):
        return patch_copy(
            solved, arrived_solved.at[sender], solved_send, solved_recv, peer, sender
        )

    def model_copy(peer, sender):
        return patch_copy(
            model_packed.at[rows_of(peer, model_peer), :],
            returned.at[rows_of(sender, model_peer), :],
            model_send,
            model_recv,
            peer,
            sender,
        )

    def pack(peer):
        for n in range(capacity):
            tile = routes[peer, 5, n]
            sigma = sigma_ref[tile] * routes[peer, 6, n].astype(jnp.float32)
            at = peer * tile_peer + n // group * tile_chunk + n % group * 4
            stage[pl.ds(at, 2), :] = science_ref[tile] * sigma
            stage[pl.ds(at + 2, 2), :] = sigma
        return stage[rows_of(peer, tile_peer), :].astype(jnp.bfloat16)

    barrier = pltpu.get_barrier_semaphore()
    peers_signal(barrier, "patch", me, patches)
    peers_signal(barrier, "visit", my_visit, visit_parts)
    own_scalars = pltpu.make_async_copy(details_ref, routes, routes_sem.at[0])
    own_scalars.start()
    if tile_chunk != 4 * group:
        stage[...] = jnp.zeros_like(stage)
    whole[rows_of(my_visit, share), :] = template_ref[...].astype(jnp.bfloat16)
    arrived_details[me] = details_ref[me]
    running[slot_count] = jnp.zeros((ROWS, LANES), jnp.float32)
    filtered[:, :, patch_columns:] = jnp.zeros((NF, start_rows, LANES), jnp.bfloat16)
    own_scalars.wait()
    arrived[rows_of(me, tile_peer), :] = pack(me)
    pl.semaphore_wait(barrier, patches - 1 + visit_parts - 1)

    for i in range(1, visit_parts):
        template_copy(lax.rem(my_visit + i, visit_parts), my_visit).start()

    def pack_and_send(peer):
        details_copy(peer, me).start()
        packed[rows_of(peer, tile_peer), :] = pack(peer)
        tile_copy(peer, me).start()

    each_peer(pack_and_send)
    for i in range(1, visit_parts):
        peer = lax.rem(my_visit + i, visit_parts)
        template_copy(peer, peer).wait_recv()

    for b in range(NF):
        filtered[b, :, :patch_columns] = jnp.dot(
            row_band_ref[b], whole[...], preferred_element_type=jnp.float32
        ).astype(jnp.bfloat16)

    def column_block(j, carry):
        at = pl.multiple_of(j * LANES, LANES)
        for b, first, indices in basis_runs():
            product = jnp.dot(
                filtered[b, :, pl.ds(at, 2 * LANES)],
                column_band_ref[:, first * LANES : (first + len(indices)) * LANES],
                preferred_element_type=jnp.float32,
            )
            for i, k in enumerate(indices):
                images[j, k * image_rows : k * image_rows + start_rows, :] = product[
                    :, i * LANES : (i + 1) * LANES
                ]
        return carry

    lax.fori_loop(0, patch_columns // LANES, column_block, 0)

    each_peer(lambda peer: details_copy(peer, peer).wait_recv())
    to_scalars = pltpu.make_async_copy(arrived_details, routes, routes_sem.at[1])
    to_scalars.start()
    to_scalars.wait()
    each_peer(lambda peer: tile_copy(peer, peer).wait_recv())

    lane = lax.broadcasted_iota(jnp.int32, (8, LANES), 1)
    eighth = lax.broadcasted_iota(jnp.int32, (8, LANES), 0)
    basis = lax.broadcasted_iota(jnp.int32, (ROWS, LANES), 0)
    part = lax.broadcasted_iota(jnp.int32, (ROWS, LANES), 1) // ROWS

    def pick(row, column):
        block = column // LANES
        shift = column % LANES
        halves = []
        for i in range(2):
            pieces = []
            for k in range(0, ROWS, 8):
                rows = pl.ds(k * image_rows + row + i, 8, stride=image_rows)
                piece = pltpu.roll(
                    jnp.where(lane >= shift, images[block, rows, :], images[block + 1, rows, :]),
                    (LANES - shift) % LANES,
                    axis=1,
                )
                if k + 8 >= NB:
                    constant = jnp.where(eighth + k == NB - 1, 1.0, 0.0)
                    piece = jnp.where(eighth + k < NB - 1, piece, constant)
                pieces.append(piece)
            halves.append(jnp.concatenate(pieces, axis=0))
        return halves

    def tile_group(g, carry):
        chunks = [
            arrived[rows_of(g * (GROUP // group) + c, tile_chunk), :].astype(jnp.float32)
            for c in range(GROUP // group)
        ]
        designs = []
        flags = []
        for t in range(GROUP):
            s = g * GROUP + t
            sender, n = s // capacity, s % capacity
            values = chunks[t // group][t % group * 4 : t % group * 4 + 4]
            halves = pick(routes[sender, 1, n], routes[sender, 2, n])
            flags.append(routes[sender, 4, n].astype(jnp.float32))
            for i in range(2):
                picked[s, i * ROWS : (i + 1) * ROWS, :] = halves[i]
            designs.append(
                jnp.concatenate(
                    [
                        jnp.where(
                            basis == RHS,
                            values[i : i + 1],
                            halves[i] * values[2 + i : 3 + i],
                        ).astype(jnp.bfloat16)
                        for i in range(2)
                    ],
                    axis=1,
                )
            )
        design = jnp.concatenate(designs, axis=0)
        products = lax.dot_general(
            design, design, (((1,), (1,)), ((), ())), preferred_element_type=jnp.float32
        )
        per = LANES // ROWS
        for t in range(GROUP):
            own = products[
                t * ROWS : (t + 1) * ROWS, (t // per) * LANES : (t // per + 1) * LANES
            ]
            carry = carry * flags[t] + jnp.where(part == t % per, own, 0.0)
            running[g * GROUP + t] = carry
        return carry

    def two_groups(h, carry):
        return tile_group(2 * h + 1, tile_group(2 * h, carry))

    lax.fori_loop(
        0, slot_count // GROUP // 2, two_groups, jnp.zeros((ROWS, LANES), jnp.float32)
    )

    def gram_of(owner):
        merged = jnp.zeros((ROWS, LANES), jnp.float32)
        for i in range(per_owner):
            v = owner * per_owner + i
            if patches <= VIS_DEV:
                folded = running[routes[0, 3, v]]
                for sender in range(1, patches):
                    folded = folded + running[routes[sender, 3, v]]
            else:
                folded = lax.fori_loop(
                    0,
                    patches,
                    lambda sender, sums: sums + running[routes[sender, 3, v]],
                    jnp.zeros((ROWS, LANES), jnp.float32),
                )
            folded = folded + pltpu.roll(folded, 2 * ROWS, axis=1)
            folded = folded + pltpu.roll(folded, ROWS, axis=1)
            merged = jnp.where(part == i, folded, merged)
        return merged

    def gram_and_send(peer):
        gram[peer] = gram_of(peer)
        gram_copy(peer, me).start()

    each_peer(lambda peer: when_owner(peer, lambda: gram_and_send(peer)))

    def solve_own():
        grams[me] = gram_of(me)
        each_peer(lambda peer: gram_copy(lax.rem(me, owners), peer).wait_recv())
        summed = jnp.sum(grams[...], axis=0)
        systems = [summed] + [
            pltpu.roll(summed, LANES - i * ROWS, axis=1) for i in range(1, per_owner)
        ]
        values = solve_systems(jnp.stack(systems, axis=0))
        merged = values[0]
        for i in range(1, per_owner):
            merged = jnp.where(
                lax.broadcasted_iota(jnp.int32, (ROWS, LANES), 1) == i, values[i], merged
            )
        solved[...] = merged
        arrived_solved[me] = merged
        each_peer(lambda peer: solved_copy(peer, me).start())

    when_owner(me, solve_own)
    each_peer(lambda peer: when_owner(peer, lambda: solved_copy(peer, peer).wait_recv()))
    for v in range(VIS_DEV):
        i = v % per_owner
        spread[v] = jnp.broadcast_to(arrived_solved[v // per_owner][:, i : i + 1], (ROWS, LANES))

    def model_of(peer):
        for n in range(capacity):
            s = peer * capacity + n
            values = spread[routes[peer, 0, n]]
            at = peer * model_peer + n // group * model_chunk + n % group * 2
            for i in range(2):
                stage[pl.ds(at + i, 1), :] = jnp.sum(
                    picked[s, i * ROWS : (i + 1) * ROWS, :] * values, axis=0, keepdims=True
                )
        return stage[rows_of(peer, model_peer), :].astype(jnp.bfloat16)

    def model_and_send(peer):
        model_packed[rows_of(peer, model_peer), :] = model_of(peer)
        model_copy(peer, me).start()

    each_peer(model_and_send)
    returned[rows_of(me, model_peer), :] = model_of(me)
    diagonal = basis == lax.broadcasted_iota(jnp.int32, (ROWS, LANES), 1)
    for v in range(VIS_DEV):
        coefficient_ref[v : v + 1, :] = jnp.sum(
            jnp.where(diagonal, spread[v], 0.0), axis=0, keepdims=True
        )

    for i in range(1, visit_parts):
        template_copy(lax.rem(my_visit + i, visit_parts), my_visit).wait_send()

    def finish(peer):
        details_copy(peer, me).wait_send()
        tile_copy(peer, me).wait_send()
        when_owner(peer, lambda: gram_copy(peer, me).wait_send())
        when_owner(me, lambda: solved_copy(peer, me).wait_send())
        model_copy(peer, me).wait_send()
        model_copy(peer, peer).wait_recv()

    each_peer(finish)
    stage[: returned.shape[0], :] = returned[...].astype(jnp.float32)

    def give_back(q, carry):
        for t in range(2 * GROUP):
            tile = q * 2 * GROUP + t
            model_ref[tile] = stage[pl.ds(place_ref[tile], 2), :]
        return carry

    lax.fori_loop(0, model_ref.shape[0] // (2 * GROUP), give_back, 0)


def per_device(science, inverse_sigma, template, destination, offsets, visit_local):
    patches = lax.axis_size("patch")
    visit_parts = lax.axis_size("visit")
    tile_count, row_count, column_count = science.shape
    capacity = max(2, 2 * tile_count // patches)
    slot_count = patches * capacity
    patch_rows, patch_columns = template.shape[1] * visit_parts, template.shape[2]
    start_rows = -(-(patch_rows - 2 * KR) // 16) * 16
    image_rows = start_rows + 8
    row_band, column_band = band_tables(start_rows, patch_rows)
    order_ids = jnp.arange(tile_count, dtype=jnp.int32)
    sort_key = visit_local * tile_count + order_ids
    same_patch = destination[:, None] == destination[None, :]
    same_visit = visit_local[:, None] == visit_local[None, :]
    tile_rank = jnp.sum(
        jnp.where(same_patch & (sort_key[None, :] < sort_key[:, None]), 1, 0), axis=1
    ).astype(jnp.int32)
    continues = jnp.any(
        same_patch & same_visit & (order_ids[None, :] < order_ids[:, None]), axis=1
    ).astype(jnp.int32)
    slot_of_tile = destination * capacity + tile_rank
    slot_ids = jnp.arange(slot_count, dtype=jnp.int32)
    holds = slot_of_tile[None, :] == slot_ids[:, None]
    per_slot = jnp.stack(
        [
            visit_local,
            offsets[:, 0],
            offsets[:, 1],
            continues,
            order_ids,
            jnp.ones_like(order_ids),
        ],
        axis=0,
    )
    per_slot = jnp.sum(jnp.where(holds[None], per_slot[:, None, :], 0), axis=2)
    per_slot = per_slot.reshape(6, patches, capacity).transpose(1, 0, 2)
    per_slot = jnp.pad(per_slot, ((0, 0), (0, 0), (0, LANES - capacity)))
    in_patch = destination[None, :] == jnp.arange(patches, dtype=jnp.int32)[:, None]
    visit_ids = jnp.arange(VIS_DEV, dtype=jnp.int32)[None, :, None]
    up_to = jnp.sum(jnp.where(in_patch[:, None] & (visit_local <= visit_ids), 1, 0), axis=2)
    present = jnp.any(in_patch[:, None] & (visit_local == visit_ids), axis=2)
    last = jnp.where(present, lax.axis_index("patch") * capacity + up_to - 1, slot_count)
    last = jnp.pad(last, ((0, 0), (0, LANES - VIS_DEV)))
    details = jnp.concatenate(
        [per_slot[:, :3], last[:, None], per_slot[:, 3:], jnp.zeros_like(last)[:, None]], axis=1
    ).astype(jnp.int32)
    group = min(GROUP, capacity)
    tile_total = slot_count // group * chunk_rows(group, 4)
    model_chunk = chunk_rows(group, 2)
    model_total = slot_count // group * model_chunk
    place_of_tile = slot_of_tile // group * model_chunk + slot_of_tile % group * 2

    owners = min(patches, VIS_DEV)
    smem = pl.BlockSpec(memory_space=pltpu.SMEM)
    vmem = pl.BlockSpec(memory_space=pltpu.VMEM)
    dma = pltpu.SemaphoreType.DMA
    wide, half = jnp.float32, jnp.bfloat16
    own_model, coefficients = pl.pallas_call(
        functools.partial(image_kernel, patches, visit_parts, capacity),
        out_shape=(
            jax.ShapeDtypeStruct(science.shape, wide),
            jax.ShapeDtypeStruct((VIS_DEV, LANES), wide),
        ),
        in_specs=[smem] + [vmem] * 6,
        out_specs=(vmem, vmem),
        scratch_shapes=[
            pltpu.VMEM((patch_rows, patch_columns), half),
            pltpu.VMEM((tile_total, LANES), half),
            pltpu.VMEM((patches, 8, LANES), jnp.int32),
            pltpu.SMEM((patches, 8, LANES), jnp.int32),
            pltpu.VMEM((tile_total, LANES), wide),
            pltpu.VMEM((tile_total, LANES), half),
            pltpu.VMEM((NF, start_rows, patch_columns + LANES), half),
            pltpu.VMEM((patch_columns // LANES, image_rows * ROWS, LANES), wide),
            pltpu.VMEM((slot_count, row_count * ROWS, LANES), wide),
            pltpu.VMEM((slot_count + 1, ROWS, LANES), wide),
            pltpu.VMEM((owners, ROWS, LANES), wide),
            pltpu.VMEM((patches, ROWS, LANES), wide),
            pltpu.VMEM((ROWS, LANES), wide),
            pltpu.VMEM((owners, ROWS, LANES), wide),
            pltpu.VMEM((VIS_DEV, ROWS, LANES), wide),
            pltpu.VMEM((model_total, LANES), half),
            pltpu.VMEM((model_total, LANES), half),
            dma((2,)),
            dma((visit_parts,)),
            dma((visit_parts,)),
            dma((patches,)),
            dma((patches,)),
            dma((patches,)),
            dma((patches,)),
            dma((owners,)),
            dma((patches,)),
            dma((patches,)),
            dma((owners,)),
            dma((patches,)),
            dma((patches,)),
        ],
        compiler_params=pltpu.CompilerParams(
            vmem_limit_bytes=VMEM_BYTES, collective_id=0, has_side_effects=True
        ),
    )(
        place_of_tile,
        template[0],
        science,
        inverse_sigma,
        details,
        row_band,
        column_band,
    )
    return (science - own_model, coefficients[:, :NB])


def solution(mesh):
    return jax.shard_map(
        per_device,
        mesh=mesh,
        in_specs=(
            P(("patch", "visit"), None, None),
            P(("patch", "visit"), None, None),
            P("patch", "visit", None),
            P(("patch", "visit")),
            P(("patch", "visit"), None),
            P(("patch", "visit")),
        ),
        out_specs=(P(("patch", "visit"), None, None), P("visit", None)),
        check_vma=False,
    )
```

time: 73.1 us -> 64 us (0.88)
  Pallas kernels: 60.9 us -> 52 us
  local copies, waits for them, and re-layouts: 8.11 us -> 2.91 us
  other arithmetic: 3 us -> 8.06 us
    pallas_call x3 -> x1, Pallas kernels: 60.9 us -> 52 us  [per_device(): pl.pallas_call(functools.partial(image_kernel, patches, visit_parts, capa...]
    squeeze x3 -> x0, local copies, waits for them, and re-layouts: 1.9 us -> none  [the longest x1 0.64 us: per_device(): arrived_details[1]]
    slice x3 -> x1, local copies, waits for them, and re-layouts: 1.73 us -> 0.01 us  [per_device(): per_slot[:, :3]]
    sub x0 -> x1, other arithmetic: none -> 1.63 us  [per_device(): return (science - own_model, coefficients[:, :NB])]
    reduce_or x0 -> x2, other arithmetic: none -> 1.14 us  [the longest x1 0.91 us: per_device(): jnp.any(same_patch & same_visit & (order_ids[None, :] < order_ids[:, None...]
    transpose x1 -> x0, local copies, waits for them, and re-layouts: 0.76 us -> none  [per_device(): arrived_details[:, :3, :capacity].transpose(1, 0, 2).reshape(3, slot_count)]
    unnamed x1 -> x3, local copies, waits for them, and re-layouts: 1.57 us -> 1.3 us
where the time goes in v2:
time: 64 us; the launch traced here: 63.7 us
  Pallas kernels  52 us (81%)
  other arithmetic  8.06 us (13%)
  local copies, waits for them, and re-layouts  2.91 us (5%)
  between operations  0.72 us (1%)
    pallas_call x1, Pallas kernels, per_device(): pl.pallas_call(functools.partial(image_kernel, patches, visit_parts, capa...  52 us
    sub x1, other arithmetic, per_device(): return (science - own_model, coefficients[:, :NB])  1.63 us
    another operation x3, local copies, waits for them, and re-layouts, per_device(): jnp.stack([visit_local, offsets[:, 0], offsets[:, 1], continues, order_id...  1.43 us
    unnamed x3, local copies, waits for them, and re-layouts  1.3 us

profile of v2, /device:TPU:0, one launch (start us, length us, event | category | flops | bytes accessed | tf_op | source)
XLA Modules:
  0.0 63.7 jit_solution(9750323367076781628)
XLA Ops:
  0.6 0.9 %fusion.1 = pred[128]{0:T(512)(128)(4,1)S(1)} fusion(s32[128]{0:T(128)} %param.13, s32[128]{0:T(128)} %param.11), kind=kLoop, calls=%fused_computation.8 | loop fusion | flops 98176 | bytes 1152 | tf_op jit(solution)/shard_map/reduce_or | solution.py:492
  1.6 0.7 %iota_add_fusion = s32[128]{0:T(128)S(1)} fusion(s32[128]{0:T(128)} %param.13), kind=kLoop, calls=%fused_computation.28 | loop fusion | flops 256 | bytes 1024 | tf_op jit(solution)/shard_map/add | solution.py:486
  2.2 0.9 %select_reduce_fusion.2 = s32[128]{0:T(128)S(1)} fusion(s32[128]{0:T(128)S(1)} %iota_add_fusion, s32[128]{0:T(128)} %param.11), kind=kLoop, calls=%fused_computation.6 | loop fusion | flops 81792 | bytes 1536 | tf_op jit(solution)/shard_map/reduce_sum | solution.py:489
  3.1 0.1 pad.13.clone
  3.2 1.2 %fusion.3 = (s32[128]{0:T(128)}, s32[128]{0:T(128)S(1)}) fusion(s32[128]{0:T(128)S(1)} %select_reduce_fusion.2, s32[128]{0:T(128)} %param.11), kind=kLoop, calls=%fused_computation.24 | loop fusion | flops 3072 | bytes 2048 | tf_op jit(solution)/shard_map/add | solution.py:525
  4.4 0.7 %iota_compare_fusion.4 = pred[8,128]{1,0:T(8,128)(4,1)S(1)} fusion(s32[128]{0:T(128)} %param.11), kind=kLoop, calls=%fused_computation.17 | loop fusion | flops 1024 | bytes 1536 | tf_op jit(solution)/shard_map/eq | solution.py:512
  5.1 0.8 %slice_bitcast_fusion = (s32[1,128]{1,0:T(1,128)S(1)}, s32[1,128]{1,0:T(1,128)S(1)}) fusion(s32[128,2]{0,1:T(2,128)} %param.12), kind=kLoop, calls=%fused_computation.26 | loop fusion | bytes 2048 | tf_op jit(solution)/shard_map/stack;squeeze | solution.py:498
  5.8 0.7 %stack.9 = s32[6,128]{1,0:T(8,128)S(1)} concatenate(s32[1,128]{1,0:T(1,128)} %bitcast.17, s32[1,128]{1,0:T(1,128)S(1)} %get-tuple-element.11, s32[1,128]{1,0:T(1,128)S(1)} %get-tuple-element.10, s32[1,128]{1,0:T(1,128)S(1)} %convert_bitcast_fusion, s32[1,128]{1,0:T(1,128)S(1)} %iota.37, s32[1,128]{1,0:T(1,128)S(1)} %stack_broadcast_in_dim.3), dimensions={0} | concatenate | bytes 6144 | tf_op jit(solution)/shard_map/stack | solution.py:498
  6.5 0.7 %iota_compare_fusion.2 = (pred[16,128]{1,0:T(8,128)(4,1)S(1)}, pred[16,128]{1,0:T(8,128)(4,1)S(1)}) fusion(s32[128]{0:T(128)} %param.13), kind=kLoop, calls=%fused_computation.14 | loop fusion | flops 4096 | bytes 4608 | tf_op jit(solution)/shard_map/le | solution.py:514
  7.1 0.2 and_reduce_fusion
  7.4 0.2 select_reduce_fusion.1
  7.7 0.3 select_reduce_fusion
  7.9 0.1 reshape.105
  8.0 0.0 copy-start
  8.1 0.7 %add_add_fusion.details_ref = s32[8,8,128]{2,1,0:T(8,128)} fusion(s32[8,3,128]{2,1,0:T(4,128)S(1)} %get-tuple-element.9, s32[8,1,128]{2,1,0:T(1,128)S(1)} %bitcast.16, s32[8,3,128]{2,1,0:T(4,128)S(1)} %get-tuple-element.8, s32[8]{0:T(128)S(1)} %pad.13.clone), kind=kLoop, calls=%fused_computation.10 | loop fusion | flops 24576 | bytes 61472 | tf_op jit(solution)/shard_map/concatenate | solution.py:518
  8.7 52.0 %shard_map.95 = (f32[128,2,128]{2,1,0:T(2,128)}, f32[16,128]{1,0:T(8,128)}) custom-call(s32[128]{0:T(128)} %get-tuple-element.6.place_ref, f32[64,1024]{1,0:T(8,128)} %bitcast.14, f32[128,2,128]{2,1,0:T(2,128)} %science_ref.1, f32[128,2,128]{2,1,0:T(2,128)} %sigma_ref.1, s32[8,8,128]{2,1,0:T(8,128)} %add_add_fusion.details_ref, ...), custom_call_target="tpu_custom_call" | custom-call | tf_op jit(solution)/shard_map/pallas_call | solution.py:532
  60.7 0.0 copy-done
  60.8 1.6 %sub.15 = f32[128,2,128]{2,1,0:T(2,128)} subtract(f32[128,2,128]{2,1,0:T(2,128)S(1)} %copy-done, f32[128,2,128]{2,1,0:T(2,128)} %get-tuple-element.4) | non-fusion elementwise | flops 32768 | bytes 393216 | tf_op jit(solution)/shard_map/sub | solution.py:584
  62.4 1.3 %copy.15 = f32[16,28]{1,0:T(8,128)} copy(f32[16,28]{1,0:T(8,128)} %bitcast.18) | data formatting | bytes 3584
  (8 shorter events, 0.1 us)
Async XLA Ops:
  8.0 52.7 %copy-start = (f32[128,2,128]{2,1,0:T(2,128)S(1)}, f32[128,2,128]{2,1,0:T(2,128)}, u32[]{:S(2)}) copy-start(f32[128,2,128]{2,1,0:T(2,128)} %science_ref.1) | copy-start | bytes 393220

commit v3 on v2

--- a/solution.py
+++ b/solution.py
@@ -126,23 +126,92 @@
     return jnp.where(row_id < NB, jnp.broadcast_to(solved, system.shape), 0.0)
 
 
+def make_routes(
+    patches, capacity, me, destination_ref, visit_ref, offsets_ref, details_ref, local_ref
+):
+    square = (LANES, LANES)
+    lane = lax.broadcasted_iota(jnp.int32, square, 1)
+    diagonal = lax.broadcasted_iota(jnp.int32, square, 0) == lane
+    lane_row = lane[:1]
+    slot_count = patches * capacity
+    group = min(GROUP, capacity)
+    chunk = chunk_rows(group, 2)
+
+    def column(row):
+        return jnp.sum(jnp.where(diagonal, row, 0), axis=1, keepdims=True)
+
+    destination = destination_ref[...]
+    key = (destination * VIS_DEV + visit_ref[...]) * LANES + lane_row
+    key_column = column(key)
+    pair_column = key_column // LANES
+    patch_column = key_column // (LANES * VIS_DEV)
+    earlier = (patch_column == destination) & (key_column < key)
+    slot = destination * capacity + jnp.sum(jnp.where(earlier, 1, 0), axis=0, keepdims=True)
+    slot_column = column(slot)
+    rank_column = slot_column - patch_column * capacity
+    values = [
+        pair_column - patch_column * VIS_DEV,
+        column(offsets_ref[0:1, :]),
+        column(offsets_ref[1:2, :]),
+        key_column - pair_column * LANES,
+        jnp.ones((LANES, 1), jnp.int32),
+    ]
+    place = slot // group * chunk + slot % group * 2
+    tables = []
+    for block in range(slot_count // LANES):
+        holds = slot_column == lane + block * LANES
+        visit, row, col, order, live = [
+            jnp.sum(jnp.where(holds, value, 0), axis=0, keepdims=True) for value in values
+        ]
+        follows = (visit == pltpu.roll(visit, 1, axis=1)) & (lane_row % capacity > 0) & (live > 0)
+        tables.append([visit, row, col, jnp.where(follows, 1, 0)])
+        local_ref[block] = jnp.concatenate(
+            [visit, row, col, visit, visit, order, live, place], axis=0
+        )
+    for block in range(patches * VIS_DEV // LANES):
+        found = jnp.max(
+            jnp.where(pair_column == lane + block * LANES, rank_column, -1), axis=0, keepdims=True
+        )
+        last = jnp.where(
+            found < 0, slot_count, jnp.minimum(found, capacity - 1) + me * capacity
+        )
+        for part in range(LANES // VIS_DEV):
+            details_ref[block * (LANES // VIS_DEV) + part, 1:2, :] = (
+                pltpu.roll(last, LANES - part * VIS_DEV, axis=1) if part else last
+            )
+    for patch in range(patches):
+        table = tables[patch * capacity // LANES]
+        merged = table[3]
+        for q in range(4):
+            shift = (q * capacity - patch * capacity) % LANES
+            moved = pltpu.roll(table[q], shift, axis=1) if shift else table[q]
+            merged = jnp.where(lane_row // capacity == q, moved, merged)
+        details_ref[patch, 0:1, :] = merged
+
+
 def image_kernel(
     patches,
     visit_parts,
     capacity,
-    place_ref,
+    destination_ref,
+    visit_ref,
+    offsets_ref,
     template_ref,
     science_ref,
     sigma_ref,
-    details_ref,
-    row_band_ref,
-    column_band_ref,
+    row_band_in,
+    column_band_in,
     model_ref,
     coefficient_ref,
     whole,
     arrived,
     arrived_details,
     routes,
+    details_ref,
+    local_ref,
+    local,
+    row_band_ref,
+    column_band_ref,
     stage,
     packed,
     filtered,
@@ -157,6 +226,7 @@
     model_packed,
     returned,
     routes_sem,
+    band_sem,
     template_send,
     template_recv,
     tile_send,
@@ -200,9 +270,12 @@
         else:
             pl.when(index < owners)(action)
 
-    def template_copy(peer, owner):
+    near = my_visit + 1 - 2 * lax.rem(my_visit, 2)
+    far = lax.rem(my_visit + 2, 4)
+
+    def template_copy(step, peer, owner):
         rows = whole.at[rows_of(owner, share), :]
-        return push(rows, rows, template_send.at[peer], template_recv.at[owner], "visit", peer)
+        return push(rows, rows, template_send.at[step], template_recv.at[step], "visit", peer)
 
     def patch_copy(source, target, send, recv, peer, sender):
         return push(source, target, send.at[peer], recv.at[sender], "patch", peer)
@@ -242,8 +315,9 @@
 
     def pack(peer):
         for n in range(capacity):
-            tile = routes[peer, 5, n]
-            sigma = sigma_ref[tile] * routes[peer, 6, n].astype(jnp.float32)
+            slot = peer * capacity + n
+            tile = local[slot // LANES, 5, slot % LANES]
+            sigma = sigma_ref[tile] * local[slot // LANES, 6, slot % LANES].astype(jnp.float32)
             at = peer * tile_peer + n // group * tile_chunk + n % group * 4
             stage[pl.ds(at, 2), :] = science_ref[tile] * sigma
             stage[pl.ds(at + 2, 2), :] = sigma
@@ -252,20 +326,28 @@
     barrier = pltpu.get_barrier_semaphore()
     peers_signal(barrier, "patch", me, patches)
     peers_signal(barrier, "visit", my_visit, visit_parts)
-    own_scalars = pltpu.make_async_copy(details_ref, routes, routes_sem.at[0])
+    bands = [
+        pltpu.make_async_copy(row_band_in, row_band_ref, band_sem.at[0]),
+        pltpu.make_async_copy(column_band_in, column_band_ref, band_sem.at[1]),
+    ]
+    for copy in bands:
+        copy.start()
+    whole[rows_of(my_visit, share), :] = template_ref[...].astype(jnp.bfloat16)
+    pl.semaphore_wait(barrier, patches - 1 + visit_parts - 1)
+    template_copy(0, far, my_visit).start()
+    template_copy(1, near, my_visit).start()
+
+    make_routes(patches, capacity, me, destination_ref, visit_ref, offsets_ref, details_ref, local_ref)
+    own_scalars = pltpu.make_async_copy(local_ref, local, routes_sem.at[0])
     own_scalars.start()
+    arrived_details[me] = details_ref[me]
     if tile_chunk != 4 * group:
         stage[...] = jnp.zeros_like(stage)
-    whole[rows_of(my_visit, share), :] = template_ref[...].astype(jnp.bfloat16)
-    arrived_details[me] = details_ref[me]
     running[slot_count] = jnp.zeros((ROWS, LANES), jnp.float32)
     filtered[:, :, patch_columns:] = jnp.zeros((NF, start_rows, LANES), jnp.bfloat16)
+    template_copy(0, far, far).wait_recv()
+    template_copy(2, near, far).start()
     own_scalars.wait()
-    arrived[rows_of(me, tile_peer), :] = pack(me)
-    pl.semaphore_wait(barrier, patches - 1 + visit_parts - 1)
-
-    for i in range(1, visit_parts):
-        template_copy(lax.rem(my_visit + i, visit_parts), my_visit).start()
 
     def pack_and_send(peer):
         details_copy(peer, me).start()
@@ -273,9 +355,11 @@
         tile_copy(peer, me).start()
 
     each_peer(pack_and_send)
-    for i in range(1, visit_parts):
-        peer = lax.rem(my_visit + i, visit_parts)
-        template_copy(peer, peer).wait_recv()
+    arrived[rows_of(me, tile_peer), :] = pack(me)
+    template_copy(1, near, near).wait_recv()
+    template_copy(2, near, lax.rem(near + 2, 4)).wait_recv()
+    for copy in bands:
+        copy.wait()
 
     for b in range(NF):
         filtered[b, :, :patch_columns] = jnp.dot(
@@ -340,8 +424,8 @@
             s = g * GROUP + t
             sender, n = s // capacity, s % capacity
             values = chunks[t // group][t % group * 4 : t % group * 4 + 4]
-            halves = pick(routes[sender, 1, n], routes[sender, 2, n])
-            flags.append(routes[sender, 4, n].astype(jnp.float32))
+            halves = pick(routes[sender, 0, capacity + n], routes[sender, 0, 2 * capacity + n])
+            flags.append(routes[sender, 0, 3 * capacity + n].astype(jnp.float32))
             for i in range(2):
                 picked[s, i * ROWS : (i + 1) * ROWS, :] = halves[i]
             designs.append(
@@ -377,25 +461,29 @@
         0, slot_count // GROUP // 2, two_groups, jnp.zeros((ROWS, LANES), jnp.float32)
     )
 
+    lane_half = lax.broadcasted_iota(jnp.int32, (ROWS // 2, LANES), 1)
+    diagonal = basis == lax.broadcasted_iota(jnp.int32, (ROWS, LANES), 1)
+
     def gram_of(owner):
         merged = jnp.zeros((ROWS, LANES), jnp.float32)
         for i in range(per_owner):
             v = owner * per_owner + i
             if patches <= VIS_DEV:
-                folded = running[routes[0, 3, v]]
+                folded = running[routes[0, 1, v]]
                 for sender in range(1, patches):
-                    folded = folded + running[routes[sender, 3, v]]
+                    folded = folded + running[routes[sender, 1, v]]
             else:
                 folded = lax.fori_loop(
                     0,
                     patches,
-                    lambda sender, sums: sums + running[routes[sender, 3, v]],
+                    lambda sender, sums: sums + running[routes[sender, 1, v]],
                     jnp.zeros((ROWS, LANES), jnp.float32),
                 )
             folded = folded + pltpu.roll(folded, 2 * ROWS, axis=1)
             folded = folded + pltpu.roll(folded, ROWS, axis=1)
             merged = jnp.where(part == i, folded, merged)
-        return merged
+        low = lane_half < LANES // 2
+        return jnp.where(low, merged[: ROWS // 2], pltpu.roll(merged[ROWS // 2 :], LANES // 2, axis=1))
 
     def gram_and_send(peer):
         gram[peer] = gram_of(peer)
@@ -407,15 +495,15 @@
         grams[me] = gram_of(me)
         each_peer(lambda peer: gram_copy(lax.rem(me, owners), peer).wait_recv())
         summed = jnp.sum(grams[...], axis=0)
+        summed = jnp.concatenate([summed, pltpu.roll(summed, LANES // 2, axis=1)], axis=0)
         systems = [summed] + [
             pltpu.roll(summed, LANES - i * ROWS, axis=1) for i in range(1, per_owner)
         ]
         values = solve_systems(jnp.stack(systems, axis=0))
-        merged = values[0]
-        for i in range(1, per_owner):
-            merged = jnp.where(
-                lax.broadcasted_iota(jnp.int32, (ROWS, LANES), 1) == i, values[i], merged
-            )
+        merged = jnp.zeros((1, LANES), jnp.float32)
+        for i in range(per_owner):
+            as_row = jnp.sum(jnp.where(diagonal, values[i], 0.0), axis=0, keepdims=True)
+            merged = merged + (pltpu.roll(as_row, i * ROWS, axis=1) if i else as_row)
         solved[...] = merged
         arrived_solved[me] = merged
         each_peer(lambda peer: solved_copy(peer, me).start())
@@ -424,7 +512,12 @@
     each_peer(lambda peer: when_owner(peer, lambda: solved_copy(peer, peer).wait_recv()))
     for v in range(VIS_DEV):
         i = v % per_owner
-        spread[v] = jnp.broadcast_to(arrived_solved[v // per_owner][:, i : i + 1], (ROWS, LANES))
+        as_row = arrived_solved[v // per_owner]
+        as_row = pltpu.roll(as_row, LANES - i * ROWS, axis=1) if i else as_row
+        coefficient_ref[v : v + 1, :] = as_row
+        spread[v] = jnp.broadcast_to(
+            jnp.sum(jnp.where(diagonal, as_row, 0.0), axis=1, keepdims=True), (ROWS, LANES)
+        )
 
     def model_of(peer):
         for n in range(capacity):
@@ -443,14 +536,9 @@
 
     each_peer(model_and_send)
     returned[rows_of(me, model_peer), :] = model_of(me)
-    diagonal = basis == lax.broadcasted_iota(jnp.int32, (ROWS, LANES), 1)
-    for v in range(VIS_DEV):
-        coefficient_ref[v : v + 1, :] = jnp.sum(
-            jnp.where(diagonal, spread[v], 0.0), axis=0, keepdims=True
-        )
-
-    for i in range(1, visit_parts):
-        template_copy(lax.rem(my_visit + i, visit_parts), my_visit).wait_send()
+    template_copy(0, far, my_visit).wait_send()
+    template_copy(1, near, my_visit).wait_send()
+    template_copy(2, near, far).wait_send()
 
     def finish(peer):
         details_copy(peer, me).wait_send()
@@ -466,7 +554,7 @@
     def give_back(q, carry):
         for t in range(2 * GROUP):
             tile = q * 2 * GROUP + t
-            model_ref[tile] = stage[pl.ds(place_ref[tile], 2), :]
+            model_ref[tile] = stage[pl.ds(local[0, 7, tile], 2), :]
         return carry
 
     lax.fori_loop(0, model_ref.shape[0] // (2 * GROUP), give_back, 0)
@@ -482,50 +570,11 @@
     start_rows = -(-(patch_rows - 2 * KR) // 16) * 16
     image_rows = start_rows + 8
     row_band, column_band = band_tables(start_rows, patch_rows)
-    order_ids = jnp.arange(tile_count, dtype=jnp.int32)
-    sort_key = visit_local * tile_count + order_ids
-    same_patch = destination[:, None] == destination[None, :]
-    same_visit = visit_local[:, None] == visit_local[None, :]
-    tile_rank = jnp.sum(
-        jnp.where(same_patch & (sort_key[None, :] < sort_key[:, None]), 1, 0), axis=1
-    ).astype(jnp.int32)
-    continues = jnp.any(
-        same_patch & same_visit & (order_ids[None, :] < order_ids[:, None]), axis=1
-    ).astype(jnp.int32)
-    slot_of_tile = destination * capacity + tile_rank
-    slot_ids = jnp.arange(slot_count, dtype=jnp.int32)
-    holds = slot_of_tile[None, :] == slot_ids[:, None]
-    per_slot = jnp.stack(
-        [
-            visit_local,
-            offsets[:, 0],
-            offsets[:, 1],
-            continues,
-            order_ids,
-            jnp.ones_like(order_ids),
-        ],
-        axis=0,
-    )
-    per_slot = jnp.sum(jnp.where(holds[None], per_slot[:, None, :], 0), axis=2)
-    per_slot = per_slot.reshape(6, patches, capacity).transpose(1, 0, 2)
-    per_slot = jnp.pad(per_slot, ((0, 0), (0, 0), (0, LANES - capacity)))
-    in_patch = destination[None, :] == jnp.arange(patches, dtype=jnp.int32)[:, None]
-    visit_ids = jnp.arange(VIS_DEV, dtype=jnp.int32)[None, :, None]
-    up_to = jnp.sum(jnp.where(in_patch[:, None] & (visit_local <= visit_ids), 1, 0), axis=2)
-    present = jnp.any(in_patch[:, None] & (visit_local == visit_ids), axis=2)
-    last = jnp.where(present, lax.axis_index("patch") * capacity + up_to - 1, slot_count)
-    last = jnp.pad(last, ((0, 0), (0, LANES - VIS_DEV)))
-    details = jnp.concatenate(
-        [per_slot[:, :3], last[:, None], per_slot[:, 3:], jnp.zeros_like(last)[:, None]], axis=1
-    ).astype(jnp.int32)
     group = min(GROUP, capacity)
     tile_total = slot_count // group * chunk_rows(group, 4)
-    model_chunk = chunk_rows(group, 2)
-    model_total = slot_count // group * model_chunk
-    place_of_tile = slot_of_tile // group * model_chunk + slot_of_tile % group * 2
+    model_total = slot_count // group * chunk_rows(group, 2)
 
     owners = min(patches, VIS_DEV)
-    smem = pl.BlockSpec(memory_space=pltpu.SMEM)
     vmem = pl.BlockSpec(memory_space=pltpu.VMEM)
     dma = pltpu.SemaphoreType.DMA
     wide, half = jnp.float32, jnp.bfloat16
@@ -535,29 +584,35 @@
             jax.ShapeDtypeStruct(science.shape, wide),
             jax.ShapeDtypeStruct((VIS_DEV, LANES), wide),
         ),
-        in_specs=[smem] + [vmem] * 6,
+        in_specs=[vmem] * 6 + [pl.BlockSpec(memory_space=pl.ANY)] * 2,
         out_specs=(vmem, vmem),
         scratch_shapes=[
             pltpu.VMEM((patch_rows, patch_columns), half),
             pltpu.VMEM((tile_total, LANES), half),
-            pltpu.VMEM((patches, 8, LANES), jnp.int32),
-            pltpu.SMEM((patches, 8, LANES), jnp.int32),
+            pltpu.VMEM((patches, 2, LANES), jnp.int32),
+            pltpu.SMEM((patches, 2, LANES), jnp.int32),
+            pltpu.VMEM((patches, 2, LANES), jnp.int32),
+            pltpu.VMEM((slot_count // LANES, 8, LANES), jnp.int32),
+            pltpu.SMEM((slot_count // LANES, 8, LANES), jnp.int32),
+            pltpu.VMEM(row_band.shape, half),
+            pltpu.VMEM(column_band.shape, half),
             pltpu.VMEM((tile_total, LANES), wide),
             pltpu.VMEM((tile_total, LANES), half),
             pltpu.VMEM((NF, start_rows, patch_columns + LANES), half),
             pltpu.VMEM((patch_columns // LANES, image_rows * ROWS, LANES), wide),
             pltpu.VMEM((slot_count, row_count * ROWS, LANES), wide),
             pltpu.VMEM((slot_count + 1, ROWS, LANES), wide),
-            pltpu.VMEM((owners, ROWS, LANES), wide),
-            pltpu.VMEM((patches, ROWS, LANES), wide),
-            pltpu.VMEM((ROWS, LANES), wide),
-            pltpu.VMEM((owners, ROWS, LANES), wide),
+            pltpu.VMEM((owners, ROWS // 2, LANES), wide),
+            pltpu.VMEM((patches, ROWS // 2, LANES), wide),
+            pltpu.VMEM((1, LANES), wide),
+            pltpu.VMEM((owners, 1, LANES), wide),
             pltpu.VMEM((VIS_DEV, ROWS, LANES), wide),
             pltpu.VMEM((model_total, LANES), half),
             pltpu.VMEM((model_total, LANES), half),
             dma((2,)),
-            dma((visit_parts,)),
-            dma((visit_parts,)),
+            dma((2,)),
+            dma((3,)),
+            dma((3,)),
             dma((patches,)),
             dma((patches,)),
             dma((patches,)),
@@ -573,11 +628,12 @@
             vmem_limit_bytes=VMEM_BYTES, collective_id=0, has_side_effects=True
         ),
     )(
-        place_of_tile,
+        destination.reshape(1, tile_count),
+        visit_local.reshape(1, tile_count),
+        offsets.T,
         template[0],
         science,
         inverse_sigma,
-        details,
         row_band,
         column_band,
     )

time: 64 us -> 54.3 us (0.85)
  other arithmetic: 8.06 us -> 1.63 us
  local copies, waits for them, and re-layouts: 2.91 us -> 1.3 us
  Pallas kernels: 52 us -> 50.6 us
    add x2 -> x0, other arithmetic: 1.85 us -> none  [the longest x1 1.18 us: per_device(): slot_of_tile // group * model_chunk + slot_of_tile % group * 2]
    pallas_call x1, Pallas kernels: 52 us -> 50.6 us  [per_device(): pl.pallas_call(functools.partial(image_kernel, patches, visit_parts, capa...]
    another operation x3 -> x0, local copies, waits for them, and re-layouts: 1.43 us -> none  [per_device(): jnp.stack([visit_local, offsets[:, 0], offsets[:, 1], continues, order_id...]
    reduce_sum x3 -> x0, other arithmetic: 1.4 us -> none  [the longest x1 0.91 us: per_device(): jnp.sum(jnp.where(same_patch & (sort_key[None, :] < sort_key[:, None]), 1...]
    reduce_or x2 -> x0, other arithmetic: 1.14 us -> none  [the longest x1 0.91 us: per_device(): jnp.any(same_patch & same_visit & (order_ids[None, :] < order_ids[:, None...]
    concatenate x1 -> x0, other arithmetic: 0.69 us -> none  [per_device(): jnp.concatenate([per_slot[:, :3], last[:, None], per_slot[:, 3:], jnp.zer...]
    eq x2 -> x0, other arithmetic: 0.69 us -> none  [the longest x1 0.66 us: per_device(): destination[None, :] == jnp.arange(patches, dtype=jnp.int32)[:, None]]
    le x1 -> x0, other arithmetic: 0.66 us -> none  [per_device(): visit_local <= visit_ids]
where the time goes in v3:
time: 54.3 us; the launch traced here: 54.1 us
  Pallas kernels  50.6 us (93%)
  other arithmetic  1.63 us (3%)
  local copies, waits for them, and re-layouts  1.3 us (2%)
  between operations  0.66 us (1%)
    pallas_call x1, Pallas kernels, per_device(): pl.pallas_call(functools.partial(image_kernel, patches, visit_parts, capa...  50.6 us
    sub x1, other arithmetic, per_device(): return (science - own_model, coefficients[:, :NB])  1.63 us
    unnamed x3, local copies, waits for them, and re-layouts  1.3 us

profile of v3, /device:TPU:0, one launch (start us, length us, event | category | flops | bytes accessed | tf_op | source)
XLA Modules:
  0.0 54.1 jit_solution(9246083019070252244)
XLA Ops:
  0.6 0.0 copy-start
  0.6 50.6 %shard_map.95 = (f32[128,2,128]{2,1,0:T(2,128)}, f32[16,128]{1,0:T(8,128)}) custom-call(s32[1,128]{1,0:T(1,128)} %bitcast.8, s32[1,128]{1,0:T(1,128)} %bitcast.9, s32[2,128]{1,0:T(2,128)} %bitcast.7, f32[64,1024]{1,0:T(8,128)} %bitcast.5, f32[128,2,128]{2,1,0:T(2,128)} %science_ref.1, f32[128,2,128]{2,1,0:T(2,128)} %sigma_ref.1, ...), custom_call_target="tpu_custom_call" | custom-call | tf_op jit(solution)/shard_map/pallas_call | solution.py:581
  51.2 0.0 copy-done
  51.2 1.6 %sub.3 = f32[128,2,128]{2,1,0:T(2,128)} subtract(f32[128,2,128]{2,1,0:T(2,128)S(1)} %copy-done, f32[128,2,128]{2,1,0:T(2,128)} %get-tuple-element.4) | non-fusion elementwise | flops 32768 | bytes 393216 | tf_op jit(solution)/shard_map/sub | solution.py:640
  52.8 1.3 %copy.11 = f32[16,28]{1,0:T(8,128)} copy(f32[16,28]{1,0:T(8,128)} %bitcast.6) | data formatting | bytes 3584
Async XLA Ops:
  0.6 50.6 %copy-start = (f32[128,2,128]{2,1,0:T(2,128)S(1)}, f32[128,2,128]{2,1,0:T(2,128)}, u32[]{:S(2)}) copy-start(f32[128,2,128]{2,1,0:T(2,128)} %science_ref.1) | copy-start | bytes 393220

commit v4 on v3

--- a/solution.py
+++ b/solution.py
@@ -13,7 +13,9 @@
 NB = 28
 VIS_DEV = 16
 ROWS = 32
-RHS = NB
+RHS = 27
+CONSTANT = 25
+CLASSES = 8
 GROUP = 8
 LANES = 128
 VMEM_BYTES = 60 * 1024 * 1024
@@ -55,13 +57,39 @@
     return (column_ids, row_ids, filter_runs)
 
 
-def band_tables(start_rows, patch_rows):
+ENTRIES = (
+    (0, 0, 0, 4, 0),
+    (0, 1, 4, 1, 0),
+    (1, 2, 0, 4, 0),
+    (2, 3, 0, 3, 0),
+    (3, 4, 0, 2, 0),
+    (4, 1, 0, 1, 1),
+    (5, 5, 5, 3, 0),
+    (6, 4, 5, 2, 2),
+    (7, 1, 5, 1, 2),
+    (8, 6, 8, 3, 0),
+    (9, 7, 8, 2, 0),
+    (10, 7, 8, 1, 2),
+)
+
+
+def positions():
+    column_ids, row_ids, _ = pair_layout()
+    index_of = {pair: k for k, pair in enumerate(zip(column_ids, row_ids))}
+    place = [CONSTANT] * NB
+    for b, shift, first, count, group in ENTRIES:
+        for i in range(count):
+            place[index_of[(first + i, b)]] = (group + i) * CLASSES + shift
+    return place
+
+
+def band_tables(stored_rows, patch_rows):
     values = filter_table(KR)
     taps_count = 2 * KR + 1
-    row_band = np.zeros((NF, start_rows, patch_rows), np.float32)
-    for start in range(start_rows):
-        stop = min(start + taps_count, patch_rows)
-        row_band[:, start, start:stop] = values.T[:, : stop - start]
+    row_band = np.zeros((len(ENTRIES), stored_rows, patch_rows), np.float32)
+    for e, (b, shift, _, _, _) in enumerate(ENTRIES):
+        for start in range(patch_rows - taps_count + 1):
+            row_band[e, start + shift, start : start + taps_count] = values[:, b]
     column_band = np.zeros((2 * LANES, NF, LANES), np.float32)
     for out_column in range(LANES):
         column_band[out_column : out_column + taps_count, :, out_column] = values
@@ -69,20 +97,6 @@
         jnp.asarray(row_band.astype(jnp.bfloat16)),
         jnp.asarray(column_band.reshape(2 * LANES, NF * LANES).astype(jnp.bfloat16)),
     )
-
-
-def basis_runs():
-    column_ids, row_ids, _ = pair_layout()
-    index_of = {pair: k for k, pair in enumerate(zip(column_ids, row_ids))}
-    runs = []
-    offset = 0
-    for degree in poly_degrees:
-        for second in range(degree + 1):
-            b = offset + second
-            count = degree + 1 - second
-            runs.append((b, offset, [index_of[(offset + i, b)] for i in range(count)]))
-        offset += degree + 1
-    return runs
 
 
 def chunk_rows(group, per_tile):
@@ -116,14 +130,15 @@
 def solve_systems(system):
     row_id = lax.broadcasted_iota(jnp.int32, system.shape, 1)
     column_id = lax.broadcasted_iota(jnp.int32, system.shape, 2)
-    for p in range(NB):
+    for p in positions():
         pivot_row = system[:, p : p + 1, :]
         inverse = 1.0 / system[:, p : p + 1, p : p + 1]
         factor = system[:, :, p : p + 1] * inverse
         system = jnp.where(row_id == p, system, system - factor * pivot_row)
     diagonal = jnp.sum(jnp.where(row_id == column_id, system, 0.0), axis=2, keepdims=True)
     solved = system[:, :, RHS : RHS + 1] / diagonal
-    return jnp.where(row_id < NB, jnp.broadcast_to(solved, system.shape), 0.0)
+    used = functools.reduce(jnp.logical_or, [row_id == p for p in positions()])
+    return jnp.where(used, jnp.broadcast_to(solved, system.shape), 0.0)
 
 
 def make_routes(
@@ -249,7 +264,7 @@
     model_chunk = chunk_rows(group, 2)
     model_peer = capacity // group * model_chunk
     share, patch_columns = template_ref.shape
-    start_rows = row_band_ref.shape[1]
+    stored_rows = row_band_ref.shape[1]
     image_rows = images.shape[1] // ROWS
     owners = gram.shape[0]
     per_owner = VIS_DEV // owners
@@ -344,7 +359,7 @@
     if tile_chunk != 4 * group:
         stage[...] = jnp.zeros_like(stage)
     running[slot_count] = jnp.zeros((ROWS, LANES), jnp.float32)
-    filtered[:, :, patch_columns:] = jnp.zeros((NF, start_rows, LANES), jnp.bfloat16)
+    filtered[:, :, patch_columns:] = jnp.zeros((len(ENTRIES), stored_rows, LANES), jnp.bfloat16)
     template_copy(0, far, far).wait_recv()
     template_copy(2, near, far).start()
     own_scalars.wait()
@@ -361,22 +376,23 @@
     for copy in bands:
         copy.wait()
 
-    for b in range(NF):
-        filtered[b, :, :patch_columns] = jnp.dot(
-            row_band_ref[b], whole[...], preferred_element_type=jnp.float32
+    for e in range(len(ENTRIES)):
+        filtered[e, :, :patch_columns] = jnp.dot(
+            row_band_ref[e], whole[...], preferred_element_type=jnp.float32
         ).astype(jnp.bfloat16)
 
     def column_block(j, carry):
         at = pl.multiple_of(j * LANES, LANES)
-        for b, first, indices in basis_runs():
+        for e, (_, shift, first, count, group_at) in enumerate(ENTRIES):
             product = jnp.dot(
-                filtered[b, :, pl.ds(at, 2 * LANES)],
-                column_band_ref[:, first * LANES : (first + len(indices)) * LANES],
+                filtered[e, :, pl.ds(at, 2 * LANES)],
+                column_band_ref[:, first * LANES : (first + count) * LANES],
                 preferred_element_type=jnp.float32,
             )
-            for i, k in enumerate(indices):
-                images[j, k * image_rows : k * image_rows + start_rows, :] = product[
-                    :, i * LANES : (i + 1) * LANES
+            for i in range(count):
+                base = ((group_at + i) * CLASSES + shift) * image_rows
+                images[j, base : base + image_rows, :] = product[
+                    :image_rows, i * LANES : (i + 1) * LANES
                 ]
         return carry
 
@@ -400,15 +416,17 @@
         for i in range(2):
             pieces = []
             for k in range(0, ROWS, 8):
-                rows = pl.ds(k * image_rows + row + i, 8, stride=image_rows)
+                rows = pl.ds(k * image_rows + row + i, CLASSES, stride=image_rows + 1)
                 piece = pltpu.roll(
                     jnp.where(lane >= shift, images[block, rows, :], images[block + 1, rows, :]),
                     (LANES - shift) % LANES,
                     axis=1,
                 )
-                if k + 8 >= NB:
-                    constant = jnp.where(eighth + k == NB - 1, 1.0, 0.0)
-                    piece = jnp.where(eighth + k < NB - 1, piece, constant)
+                if k + CLASSES == ROWS:
+                    kept = functools.reduce(
+                        jnp.logical_or, [eighth + k == p for p in positions()[:-1] if p >= k]
+                    )
+                    piece = jnp.where(kept, piece, jnp.where(eighth + k == CONSTANT, 1.0, 0.0))
                 pieces.append(piece)
             halves.append(jnp.concatenate(pieces, axis=0))
         return halves
@@ -462,7 +480,10 @@
     )
 
     lane_half = lax.broadcasted_iota(jnp.int32, (ROWS // 2, LANES), 1)
-    diagonal = basis == lax.broadcasted_iota(jnp.int32, (ROWS, LANES), 1)
+    basis_lane = lax.broadcasted_iota(jnp.int32, (ROWS, LANES), 1)
+    diagonal = functools.reduce(
+        jnp.logical_or, [(basis == p) & (basis_lane == k) for k, p in enumerate(positions())]
+    )
 
     def gram_of(owner):
         merged = jnp.zeros((ROWS, LANES), jnp.float32)
@@ -567,9 +588,9 @@
     capacity = max(2, 2 * tile_count // patches)
     slot_count = patches * capacity
     patch_rows, patch_columns = template.shape[1] * visit_parts, template.shape[2]
-    start_rows = -(-(patch_rows - 2 * KR) // 16) * 16
-    image_rows = start_rows + 8
-    row_band, column_band = band_tables(start_rows, patch_rows)
+    image_rows = -(-(patch_rows - 2 * KR + CLASSES - 1) // 8) * 8
+    stored_rows = -(-image_rows // 16) * 16
+    row_band, column_band = band_tables(stored_rows, patch_rows)
     group = min(GROUP, capacity)
     tile_total = slot_count // group * chunk_rows(group, 4)
     model_total = slot_count // group * chunk_rows(group, 2)
@@ -598,7 +619,7 @@
             pltpu.VMEM(column_band.shape, half),
             pltpu.VMEM((tile_total, LANES), wide),
             pltpu.VMEM((tile_total, LANES), half),
-            pltpu.VMEM((NF, start_rows, patch_columns + LANES), half),
+            pltpu.VMEM((len(ENTRIES), stored_rows, patch_columns + LANES), half),
             pltpu.VMEM((patch_columns // LANES, image_rows * ROWS, LANES), wide),
             pltpu.VMEM((slot_count, row_count * ROWS, LANES), wide),
             pltpu.VMEM((slot_count + 1, ROWS, LANES), wide),

time: 54.3 us -> 54.2 us (level)
  no operation moved by 1% of the time
where the time goes in v4:
time: 54.2 us; the launch traced here: 54 us
  Pallas kernels  50.4 us (93%)
  other arithmetic  1.63 us (3%)
  local copies, waits for them, and re-layouts  1.3 us (2%)
  between operations  0.66 us (1%)
    pallas_call x1, Pallas kernels, per_device(): pl.pallas_call(functools.partial(image_kernel, patches, visit_parts, capa...  50.4 us
    sub x1, other arithmetic, per_device(): return (science - own_model, coefficients[:, :NB])  1.63 us
    unnamed x3, local copies, waits for them, and re-layouts  1.3 us

profile of v4, /device:TPU:0, one launch (start us, length us, event | category | flops | bytes accessed | tf_op | source)
XLA Modules:
  0.0 54.0 jit_solution(12785049163198024926)
XLA Ops:
  0.6 0.0 copy-start
  0.6 50.4 %shard_map.95 = (f32[128,2,128]{2,1,0:T(2,128)}, f32[16,128]{1,0:T(8,128)}) custom-call(s32[1,128]{1,0:T(1,128)} %bitcast.8, s32[1,128]{1,0:T(1,128)} %bitcast.9, s32[2,128]{1,0:T(2,128)} %bitcast.7, f32[64,1024]{1,0:T(8,128)} %bitcast.5, f32[128,2,128]{2,1,0:T(2,128)} %science_ref.1, f32[128,2,128]{2,1,0:T(2,128)} %sigma_ref.1, ...), custom_call_target="tpu_custom_call" | custom-call | tf_op jit(solution)/shard_map/pallas_call | solution.py:602
  51.1 0.0 copy-done
  51.1 1.6 %sub.3 = f32[128,2,128]{2,1,0:T(2,128)} subtract(f32[128,2,128]{2,1,0:T(2,128)S(1)} %copy-done, f32[128,2,128]{2,1,0:T(2,128)} %get-tuple-element.4) | non-fusion elementwise | flops 32768 | bytes 393216 | tf_op jit(solution)/shard_map/sub | solution.py:661
  52.7 1.3 %copy.11 = f32[16,28]{1,0:T(8,128)} copy(f32[16,28]{1,0:T(8,128)} %bitcast.6) | data formatting | bytes 3584
Async XLA Ops:
  0.6 50.5 %copy-start = (f32[128,2,128]{2,1,0:T(2,128)S(1)}, f32[128,2,128]{2,1,0:T(2,128)}, u32[]{:S(2)}) copy-start(f32[128,2,128]{2,1,0:T(2,128)} %science_ref.1) | copy-start | bytes 393220

commit v5 on v3

--- a/solution.py
+++ b/solution.py
@@ -115,14 +115,19 @@
 
 def solve_systems(system):
     row_id = lax.broadcasted_iota(jnp.int32, system.shape, 1)
-    column_id = lax.broadcasted_iota(jnp.int32, system.shape, 2)
-    for p in range(NB):
-        pivot_row = system[:, p : p + 1, :]
-        inverse = 1.0 / system[:, p : p + 1, p : p + 1]
-        factor = system[:, :, p : p + 1] * inverse
-        system = jnp.where(row_id == p, system, system - factor * pivot_row)
-    diagonal = jnp.sum(jnp.where(row_id == column_id, system, 0.0), axis=2, keepdims=True)
-    solved = system[:, :, RHS : RHS + 1] / diagonal
+    for p in range(0, NB, 2):
+        q = p + 1
+        top, low = system[:, p : p + 1, :], system[:, q : q + 1, :]
+        a, b = system[:, p : p + 1, p : p + 1], system[:, p : p + 1, q : q + 1]
+        c, d = system[:, q : q + 1, p : p + 1], system[:, q : q + 1, q : q + 1]
+        ratio = c / a
+        schur = 1.0 / (d - ratio * b)
+        low = (low - ratio * top) * schur
+        top = (top - b * low) / a
+        left, right = system[:, :, p : p + 1], system[:, :, q : q + 1]
+        reduced = system - left * top - right * low
+        system = jnp.where(row_id == p, top, jnp.where(row_id == q, low, reduced))
+    solved = system[:, :, RHS : RHS + 1]
     return jnp.where(row_id < NB, jnp.broadcast_to(solved, system.shape), 0.0)
 
 

time: 54.3 us -> 55.2 us (1.017)
  Pallas kernels: 50.6 us -> 51.3 us
    pallas_call x1, Pallas kernels: 50.6 us -> 51.3 us  [per_device(): pl.pallas_call(functools.partial(image_kernel, patches, visit_parts, capa...]
where the time goes in v5:
time: 55.2 us; the launch traced here: 54.9 us
  Pallas kernels  51.3 us (93%)
  other arithmetic  1.63 us (3%)
  local copies, waits for them, and re-layouts  1.3 us (2%)
  between operations  0.66 us (1%)
    pallas_call x1, Pallas kernels, per_device(): pl.pallas_call(functools.partial(image_kernel, patches, visit_parts, capa...  51.3 us
    sub x1, other arithmetic, per_device(): return (science - own_model, coefficients[:, :NB])  1.63 us
    unnamed x3, local copies, waits for them, and re-layouts  1.3 us

profile of v5, /device:TPU:0, one launch (start us, length us, event | category | flops | bytes accessed | tf_op | source)
XLA Modules:
  0.0 54.9 jit_solution(11123778757241119343)
XLA Ops:
  0.6 0.0 copy-start
  0.6 51.3 %shard_map.95 = (f32[128,2,128]{2,1,0:T(2,128)}, f32[16,128]{1,0:T(8,128)}) custom-call(s32[1,128]{1,0:T(1,128)} %bitcast.8, s32[1,128]{1,0:T(1,128)} %bitcast.9, s32[2,128]{1,0:T(2,128)} %bitcast.7, f32[64,1024]{1,0:T(8,128)} %bitcast.5, f32[128,2,128]{2,1,0:T(2,128)} %science_ref.1, f32[128,2,128]{2,1,0:T(2,128)} %sigma_ref.1, ...), custom_call_target="tpu_custom_call" | custom-call | tf_op jit(solution)/shard_map/pallas_call | solution.py:586
  51.9 0.0 copy-done
  52.0 1.6 %sub.3 = f32[128,2,128]{2,1,0:T(2,128)} subtract(f32[128,2,128]{2,1,0:T(2,128)S(1)} %copy-done, f32[128,2,128]{2,1,0:T(2,128)} %get-tuple-element.4) | non-fusion elementwise | flops 32768 | bytes 393216 | tf_op jit(solution)/shard_map/sub | solution.py:645
  53.6 1.3 %copy.11 = f32[16,28]{1,0:T(8,128)} copy(f32[16,28]{1,0:T(8,128)} %bitcast.6) | data formatting | bytes 3584
Async XLA Ops:
  0.6 51.3 %copy-start = (f32[128,2,128]{2,1,0:T(2,128)S(1)}, f32[128,2,128]{2,1,0:T(2,128)}, u32[]{:S(2)}) copy-start(f32[128,2,128]{2,1,0:T(2,128)} %science_ref.1) | copy-start | bytes 393220
